TPU v7x, 32 devices: a whole 2x2x4 slice. The times are simulated.
32 devices in a mesh: dp: 8 (over z, x), tensor: 4 (over y, core).
Axes of the slice: x: 2, y: 2, z: 4, core: 2. Of those that a mesh axis runs over, the one named last changes fastest.
Arguments:
- tokens: bfloat16 [8192, 2048], P('dp'), may hold values from -6 to 6
- seq_lengths: int32 [8, 5], P('dp'), may hold values from 1 to 512, 1024 in all within a row
- qkv_weight: bfloat16 [3, 2048, 2048], P(None, None, 'tensor'), may hold values from -0.125 to 0.125
- qkv_bias: bfloat16 [3, 2048], P(None, 'tensor'), may hold values from -4 to 4
- out_weight: bfloat16 [2048, 2048], P('tensor'), may hold values from -0.375 to 0.375
- gate_up_weight: bfloat16 [2, 2048, 5632], P(None, None, 'tensor'), may hold values from -0.125 to 0.125
- down_weight: bfloat16 [5632, 2048], P('tensor'), may hold values from -0.078125 to 0.078125
- norm_gains: float32 [2, 2048], replicated, may hold values from 0.25 to 1.75
- norm_shifts: float32 [2, 2048], replicated, may hold values from -2 to 2
- cotangent: bfloat16 [8192, 2048], P('dp'), may hold values from -6 to 6
Outputs:
- block_out: bfloat16 [8192, 2048], P(('dp', 'tensor'))
- input_grad: float32 [8192, 2048], P(('dp', 'tensor'))
- qkv_weight_grad: float32 [3, 2048, 2048], P(None, 'dp', 'tensor')
- qkv_bias_grad: float32 [3, 2048], replicated
- out_weight_grad: float32 [2048, 2048], P('tensor', 'dp')
- gate_up_weight_grad: float32 [2, 2048, 5632], P(None, 'dp', 'tensor')
- down_weight_grad: float32 [5632, 2048], P('tensor', 'dp')
- norm_gains_grad: float32 [2, 2048], replicated
- norm_shifts_grad: float32 [2, 2048], replicated
All inputs are finite; a program needn't handle non-finite values.
Results may differ from a plain program's by a relative error of at most 0.018.
Values may be sent and summed in bfloat16 or wider, within the bound.
A program may use at most 384 MiB of HBM per device.

v0:
```python
import jax
import jax.numpy as jnp
from jax import lax
from jax.sharding import PartitionSpec as P

HD = 64


def norm_parts(values):
    centred = values - jnp.mean(values, axis=-1, keepdims=True)
    inverse = lax.rsqrt(jnp.mean(centred * centred, axis=-1, keepdims=True) + 1e-05)
    return (centred * inverse, inverse)


def norm_back(unit, inverse, gain_row, grad_rows):
    scaled = grad_rows * gain_row
    return inverse * (
        scaled
        - jnp.mean(scaled, axis=-1, keepdims=True)
        - unit * jnp.mean(scaled * unit, axis=-1, keepdims=True)
    )


def positions(lengths, row_count):
    indices = jnp.arange(row_count, dtype=jnp.int32)
    ends_at = jnp.cumsum(lengths, dtype=jnp.int32)
    passed = indices[:, None] >= ends_at[None, :]
    segment = jnp.sum(passed.astype(jnp.int32), axis=1, dtype=jnp.int32)
    begins = jnp.sum(jnp.where(passed, lengths[None, :], 0), axis=1, dtype=jnp.int32)
    places = (indices - begins).astype(jnp.float32)
    halfway = HD // 8
    rates = 10000.0 ** (-(jnp.arange(halfway, dtype=jnp.float32) / halfway))
    angles = places[:, None] * rates[None, :]
    return (jnp.cos(angles), jnp.sin(angles), segment, indices)


def rotate(values, cosine, sine):
    halfway = cosine.shape[-1]
    first_half = values[..., :halfway]
    second_half = values[..., halfway : 2 * halfway]
    cos_rows = cosine[:, None, :]
    sin_rows = sine[:, None, :]
    return jnp.concatenate(
        [
            first_half * cos_rows - second_half * sin_rows,
            second_half * cos_rows + first_half * sin_rows,
            values[..., 2 * halfway :],
        ],
        axis=-1,
    )


def attend_forward(queries, keys_low, values_low, segment, indices, scale):
    row_count, heads, width = queries.shape
    block_rows = min(512, row_count)
    blocks = row_count // block_rows

    def one_block(packed):
        query_rows, query_seg, query_idx = packed
        scores = (
            jnp.einsum("qhd,khd->hqk", query_rows, keys_low, preferred_element_type=jnp.float32)
            * scale
        )
        allowed = (query_seg[:, None] == segment[None, :]) & (
            indices[None, :] <= query_idx[:, None]
        )
        masked = jnp.where(allowed[None], scores, -1e30)
        highest_score = jnp.max(masked, axis=-1, keepdims=True)
        shifted = jnp.exp(masked - highest_score)
        totals = jnp.sum(shifted, axis=-1, keepdims=True)
        probs = shifted / totals
        result = jnp.einsum(
            "hqk,khd->qhd",
            probs.astype(jnp.bfloat16),
            values_low,
            preferred_element_type=jnp.float32,
        )
        return (result.astype(jnp.bfloat16), (highest_score + jnp.log(totals))[..., 0])

    outputs, log_totals = lax.map(
        one_block,
        (
            queries.reshape(blocks, block_rows, heads, width),
            segment.reshape(blocks, block_rows),
            indices.reshape(blocks, block_rows),
        ),
    )
    return (outputs.reshape(row_count, heads * width), log_totals)


def attend_backward(queries, keys_low, values_low, grad_heads, log_totals, segment, indices, scale):
    row_count, heads, width = queries.shape
    block_rows = min(512, row_count)
    blocks = row_count // block_rows

    def one_block(carry, packed):
        keys_grad, values_grad = carry
        query_rows, grad_rows, log_rows, query_seg, query_idx = packed
        scores = (
            jnp.einsum("qhd,khd->hqk", query_rows, keys_low, preferred_element_type=jnp.float32)
            * scale
        )
        allowed = (query_seg[:, None] == segment[None, :]) & (
            indices[None, :] <= query_idx[:, None]
        )
        probs = jnp.where(allowed[None], jnp.exp(scores - log_rows[..., None]), 0.0)
        prob_grad = jnp.einsum(
            "qhd,khd->hqk", grad_rows, values_low, preferred_element_type=jnp.float32
        )
        inner = jnp.sum(probs * prob_grad, axis=-1, keepdims=True)
        score_grad = (probs * (prob_grad - inner)).astype(jnp.bfloat16)
        query_grad = (
            jnp.einsum("hqk,khd->qhd", score_grad, keys_low, preferred_element_type=jnp.float32)
            * scale
        )
        keys_grad = (
            keys_grad
            + jnp.einsum("hqk,qhd->khd", score_grad, query_rows, preferred_element_type=jnp.float32)
            * scale
        )
        values_grad = values_grad + jnp.einsum(
            "hqk,qhd->khd",
            probs.astype(jnp.bfloat16),
            grad_rows,
            preferred_element_type=jnp.float32,
        )
        return ((keys_grad, values_grad), query_grad)

    zeros_kv = jnp.zeros(keys_low.shape, jnp.float32)
    (keys_grad, values_grad), query_grad = lax.scan(
        one_block,
        (zeros_kv, zeros_kv),
        (
            queries.reshape(blocks, block_rows, heads, width),
            grad_heads.reshape(blocks, block_rows, heads, width),
            log_totals,
            segment.reshape(blocks, block_rows),
            indices.reshape(blocks, block_rows),
        ),
    )
    return (query_grad.reshape(row_count, heads, width), keys_grad, values_grad)


def body(
    tokens,
    seq_lengths,
    qkv_weight,
    qkv_bias,
    out_weight,
    gate_up_weight,
    down_weight,
    norm_gains,
    norm_shifts,
    cotangent,
):
    row_count = tokens.shape[0]
    full_width = tokens.shape[1]
    share = row_count // lax.axis_size("tensor")
    first_row = lax.axis_index("tensor") * share
    local_width = qkv_weight.shape[2]
    local_heads = local_width // HD
    scale = HD ** (-0.5)

    def own_rows(values):
        return lax.dynamic_slice_in_dim(values, first_row, share, 0)

    inputs = tokens.astype(jnp.float32)
    cosine, sine, segment, indices = positions(seq_lengths[0], row_count)
    unit_first, inverse_first = norm_parts(inputs)
    normed = (unit_first * norm_gains[0] + norm_shifts[0]).astype(jnp.bfloat16)
    projected = jnp.einsum("td,kde->kte", normed, qkv_weight, preferred_element_type=jnp.float32)
    projected = projected + qkv_bias.astype(jnp.float32)[:, None, :]
    queries = rotate(projected[0].reshape(row_count, local_heads, HD), cosine, sine).astype(
        jnp.bfloat16
    )
    keys_low = rotate(projected[1].reshape(row_count, local_heads, HD), cosine, sine).astype(
        jnp.bfloat16
    )
    values_low = projected[2].reshape(row_count, local_heads, HD).astype(jnp.bfloat16)
    heads_out, log_totals = attend_forward(queries, keys_low, values_low, segment, indices, scale)
    attended = lax.psum(
        jnp.dot(heads_out, out_weight, preferred_element_type=jnp.float32), "tensor"
    )
    residual = inputs + attended
    unit_second, inverse_second = norm_parts(residual)
    second = (unit_second * norm_gains[1] + norm_shifts[1]).astype(jnp.bfloat16)
    gate_up = jnp.einsum("td,kdf->ktf", second, gate_up_weight, preferred_element_type=jnp.float32)
    gate = gate_up[0]
    upper = gate_up[1]
    sigmoid_gate = jax.nn.sigmoid(gate)
    activated = gate * sigmoid_gate
    hidden = (activated * upper).astype(jnp.bfloat16)
    branch = lax.psum(
        jnp.dot(hidden, down_weight, preferred_element_type=jnp.float32).astype(jnp.bfloat16),
        "tensor",
    ).astype(jnp.float32)
    block_out = own_rows(residual + branch).astype(jnp.bfloat16)
    down_grad = jnp.einsum("tf,td->fd", hidden, cotangent, preferred_element_type=jnp.float32)
    hidden_grad = jnp.einsum(
        "td,fd->tf", cotangent, down_weight, preferred_element_type=jnp.float32
    )
    gate_grad = hidden_grad * upper * (sigmoid_gate * (1.0 + gate * (1.0 - sigmoid_gate)))
    upper_grad = hidden_grad * activated
    gate_up_low = jnp.stack([gate_grad, upper_grad]).astype(jnp.bfloat16)
    gate_up_grad = jnp.einsum(
        "td,ktf->kdf", second, gate_up_low, preferred_element_type=jnp.float32
    )
    second_grad = lax.psum(
        jnp.einsum("ktf,kdf->td", gate_up_low, gate_up_weight, preferred_element_type=jnp.float32),
        "tensor",
    )
    residual_grad = cotangent.astype(jnp.float32) + norm_back(
        unit_second, inverse_second, norm_gains[1], second_grad
    )
    residual_grad_own = own_rows(residual_grad)
    second_grad_own = own_rows(second_grad)
    unit_second_own = own_rows(unit_second)
    residual_low = residual_grad.astype(jnp.bfloat16)
    gain_second = jnp.sum(second_grad_own * unit_second_own, axis=0)
    shift_second = jnp.sum(second_grad_own, axis=0)
    out_grad = jnp.einsum("te,td->ed", heads_out, residual_low, preferred_element_type=jnp.float32)
    heads_grad = jnp.einsum(
        "td,ed->te", residual_low, out_weight, preferred_element_type=jnp.float32
    ).astype(jnp.bfloat16)
    query_grad, key_grad, value_grad = attend_backward(
        queries,
        keys_low,
        values_low,
        heads_grad.reshape(row_count, local_heads, HD),
        log_totals,
        segment,
        indices,
        scale,
    )
    query_grad = rotate(query_grad, cosine, -sine).reshape(row_count, local_width)
    key_grad = rotate(key_grad, cosine, -sine).reshape(row_count, local_width)
    projected_low = jnp.stack(
        [query_grad, key_grad, value_grad.reshape(row_count, local_width)]
    ).astype(jnp.bfloat16)
    qkv_grad = jnp.einsum("td,kte->kde", normed, projected_low, preferred_element_type=jnp.float32)
    bias_local = jnp.sum(projected_low, axis=1, dtype=jnp.float32)
    normed_grad_own = lax.psum_scatter(
        jnp.einsum(
            "kte,kde->td", projected_low, qkv_weight, preferred_element_type=jnp.float32
        ).astype(jnp.bfloat16),
        "tensor",
        scatter_dimension=0,
        tiled=True,
    ).astype(jnp.float32)
    unit_first_own = own_rows(unit_first)
    input_grad = residual_grad_own + norm_back(
        unit_first_own, own_rows(inverse_first), norm_gains[0], normed_grad_own
    )
    gain_first = jnp.sum(normed_grad_own * unit_first_own, axis=0)
    shift_first = jnp.sum(normed_grad_own, axis=0)
    bias_placed = lax.dynamic_update_slice(
        jnp.zeros((3, full_width), jnp.float32),
        bias_local,
        (0, lax.axis_index("tensor") * local_width),
    )
    gains_grad, shifts_grad, bias_grad = lax.psum(
        (jnp.stack([gain_first, gain_second]), jnp.stack([shift_first, shift_second]), bias_placed),
        ("dp", "tensor"),
    )
    qkv_part, out_part, gate_up_part, down_part = (
        lax.psum_scatter(
            qkv_grad.astype(jnp.bfloat16), "dp", scatter_dimension=1, tiled=True
        ).astype(jnp.float32),
        lax.psum_scatter(
            out_grad.astype(jnp.bfloat16), "dp", scatter_dimension=1, tiled=True
        ).astype(jnp.float32),
        lax.psum_scatter(
            gate_up_grad.astype(jnp.bfloat16), "dp", scatter_dimension=1, tiled=True
        ).astype(jnp.float32),
        lax.psum_scatter(
            down_grad.astype(jnp.bfloat16), "dp", scatter_dimension=1, tiled=True
        ).astype(jnp.float32),
    )
    return (
        block_out,
        input_grad,
        qkv_part,
        bias_grad,
        out_part,
        gate_up_part,
        down_part,
        gains_grad,
        shifts_grad,
    )


def solution(mesh):
    return jax.shard_map(
        body,
        mesh=mesh,
        in_specs=(
            P("dp", None),
            P("dp", None),
            P(None, None, "tensor"),
            P(None, "tensor"),
            P("tensor", None),
            P(None, None, "tensor"),
            P("tensor", None),
            P(),
            P(),
            P("dp", None),
        ),
        out_specs=(
            P(("dp", "tensor"), None),
            P(("dp", "tensor"), None),
            P(None, "dp", "tensor"),
            P(),
            P("tensor", "dp"),
            P(None, "dp", "tensor"),
            P("tensor", "dp"),
            P(),
            P(),
        ),
        check_vma=False,
    )
```

profile of v0, /device:TPU:0, one launch (start us, length us, event | category | flops | bytes accessed | tf_op | source)
XLA Modules:
  0.0 1100.8 jit_solution(17812106369436827937)
XLA Ops:
  13.4 10.4 add_bitcast_fusion
  36.2 31.8 %while.28 = (s32[]{:T(128)}, bf16[2,512,8,64]{1,3,2,0:T(8,128)(2,1)S(1)}, f32[2,8,512]{2,1,0:T(8,128)S(1)}, s32[2,512]{1,0:T(2,128)S(1)}, s32[1024]{0:T(1024)S(1...) while((s32[]{:T(128)}, ...), condition=%wide.region_8.9_spmd.clone, body=%wide.region_5.8_spmd.clone.sunk | while | flops 1125904384 | bytes 55722108 | solution.py:80
  37.3 4.9 fusion.115
  42.1 4.2 fusion.116
  46.4 5.9 fusion.117
  52.9 4.9 fusion.115
  57.8 4.2 fusion.116
  62.0 5.9 fusion.117
  69.3 5.6 fusion.72
  75.0 155.7 %all-reduce.5.cloned.1.call-done = f32[1024,2048]{1,0:T(8,128)} async-done(((f32[1024,2048]{1,0:T(8,128)}), f32[1024,2048]{1,0:T(8,128)}) %all-reduce.5.cloned.1.call-update) | async-done | bytes 8388624 | tf_op jit(solution)/shard_map/psum | solution.py:181
  230.7 7.8 fusion.68
  242.4 3.2 copy-done.9
  245.6 17.4 %convolution_bitcast_fusion = f32[2,1024,1408]{2,1,0:T(8,128)} fusion(bf16[2,2048,1408]{2,1,0:T(8,128)(2,1)} %param.19, f32[1024,2048]{1,0:T(8,128)S(1)} %subtract_multiply_fusion, f32[2048]{0:T(1024)S(1)} %bitcast.206, f32[2048]{0:T(1024)S(1)} %bitcast.198), kind=kOutput, calls=%fused_computation.65 | convolution fusion | flops 11817451520 | bytes 31473664 | tf_op jit(solution)/shard_map/td,kdf->ktf/dot_general | solution.py:187
  263.1 15.5 %fusion.46 = (bf16[1,1024,1408]{2,1,0:T(8,128)(2,1)S(1)}, bf16[1,1024,1408]{2,1,0:T(8,128)(2,1)S(1)}, bf16[1024,1408]{1,0:T(8,128)(2,1)}) fusion(f32[2,1024,1408]{2,1,0:T(8,128)} %convolution_bitcast_fusion, bf16[1024,2048]{1,0:T(8,128)(2,1)} %param.23, bf16[1408,2048]{1,0:T(8,128)(2,1)} %param.20), kind=kOutput, calls=%fused_computation.90 | convolution fusion | flops 5927206912 | bytes 30146560 | tf_op jit(solution)/shard_map/td,fd->tf/dot_general | solution.py:199
  281.1 17.3 %convolution_bitcast_fusion.1 = f32[1024,2048]{1,0:T(8,128)} fusion(bf16[2,2048,1408]{2,1,0:T(8,128)(2,1)} %param.19, bf16[1,1024,1408]{2,1,0:T(8,128)(2,1)S(1)} %get-tuple-element.326, bf16[1,1024,1408]{2,1,0:T(8,128)(2,1)S(1)} %get-tuple-element.325), kind=kOutput, calls=%fused_computation.77 | convolution fusion | flops 11814043648 | bytes 25690112 | tf_op jit(solution)/shard_map/ktf,kdf->td/dot_general | solution.py:209
  298.4 10.9 convolution_convert_fusion.1
  309.4 142.1 %all-reduce.9.cloned.1.call-done = f32[1024,2048]{1,0:T(8,128)} async-done(((f32[1024,2048]{1,0:T(8,128)}), f32[1024,2048]{1,0:T(8,128)}) %all-reduce.9.cloned.1.call-update) | async-done | bytes 8388624 | tf_op jit(solution)/shard_map/psum | solution.py:208
  451.6 7.2 multiply_reduce_fusion.3
  461.8 5.3 multiply_add_fusion
  467.1 3.2 copy-done.10
  470.3 3.7 convolution_convert_fusion.2
  474.1 10.7 convolution_convert_fusion
  484.8 5.7 fusion.56
  493.9 123.6 %while.29 = (s32[]{:T(128)}, f32[1024,8,64]{0,2,1:T(8,128)}, f32[1024,8,64]{0,2,1:T(8,128)}, f32[2,512,8,64]{1,0,3,2:T(2,128)}, bf16[2,512,8,64]{1,3,2,0:T(8,128...) while((s32[]{:T(128)}, f32[1024,8,64]{0,2,1:T(8,128)}, ...), condition=%wide.region_18.19_spmd.clone, body=%wide.region_16.18_spmd.clone.sunk | while | flops 2726555648 | bytes 200376608 | solution.py:130
  494.5 3.8 fusion.127
  498.3 11.0 %multiply_reduce_fusion.6 = (f32[8,512]{1,0:T(8,128)S(1)}, f32[8,512,1024]{2,1,0:T(8,128)}) fusion(f32[8,512,1024]{2,1,0:T(8,128)S(1)} %fusion.127, f32[8,512]{1,0:T(8,128)S(1)} %dynamic-slice_bitcast_fusion.2, bf16[1024,8,64]{0,2,1:T(8,128)(2,1)} %get-tuple-element.562, bf16[2,512,8,64]{1,3,2,0:T(8,128)(2,1)} %get-tuple-element.558, ...), kind=kOutput, calls=%fused_computation.23.clone.1 | convolution fusion | flops 557838336 | bytes 35684356 | tf_op jit(solution)/shard_map/while/body/eval_jaxpr/qhd,khd->hqk/dot_general | solution.py:100
  509.3 9.6 multiply_convert_fusion.5
  518.9 9.0 bitcast_add_fusion.5
  527.9 4.0 fusion.129
  535.9 19.5 %dynamic_update_slice.27 = f32[2,512,8,64]{1,0,3,2:T(2,128)} dynamic-update-slice(f32[2,512,8,64]{1,0,3,2:T(2,128)} %get-tuple-element.543, f32[1,512,8,64]{1,0,3,2:T(1,128)S(1)} %copy.87, s32[]{:T(128)S(6)} %copy.109, s32[]{:T(128)} %constant.48.clone.1..sunk, s32[]{:T(128)} %constant.48.clone.1..sunk, s32[]{:T(128)} %constant.48.clone.1..sunk) | dynamic-update-slice | bytes 2097156 | tf_op jit(solution)/shard_map/while/body/jit(dynamic_update_index_in_dim)/dynamic_update_slice | solution.py:130
  556.1 3.8 fusion.127
  559.9 11.0 %multiply_reduce_fusion.6 = (f32[8,512]{1,0:T(8,128)S(1)}, f32[8,512,1024]{2,1,0:T(8,128)}) fusion(f32[8,512,1024]{2,1,0:T(8,128)S(1)} %fusion.127, f32[8,512]{1,0:T(8,128)S(1)} %dynamic-slice_bitcast_fusion.2, bf16[1024,8,64]{0,2,1:T(8,128)(2,1)} %get-tuple-element.562, bf16[2,512,8,64]{1,3,2,0:T(8,128)(2,1)} %get-tuple-element.558, ...), kind=kOutput, calls=%fused_computation.23.clone.1 | convolution fusion | flops 557838336 | bytes 35684356 | tf_op jit(solution)/shard_map/while/body/eval_jaxpr/qhd,khd->hqk/dot_general | solution.py:100
  570.9 9.5 multiply_convert_fusion.5
  580.4 9.6 bitcast_add_fusion.5
  590.0 4.0 fusion.129
  598.0 19.5 %dynamic_update_slice.27 = f32[2,512,8,64]{1,0,3,2:T(2,128)} dynamic-update-slice(f32[2,512,8,64]{1,0,3,2:T(2,128)} %get-tuple-element.543, f32[1,512,8,64]{1,0,3,2:T(1,128)S(1)} %copy.87, s32[]{:T(128)S(6)} %copy.109, s32[]{:T(128)} %constant.48.clone.1..sunk, s32[]{:T(128)} %constant.48.clone.1..sunk, s32[]{:T(128)} %constant.48.clone.1..sunk) | dynamic-update-slice | bytes 2097156 | tf_op jit(solution)/shard_map/while/body/jit(dynamic_update_index_in_dim)/dynamic_update_slice | solution.py:130
  617.6 3.5 reshape.367
  631.9 11.1 %bitcast_convert_fusion = bf16[1024,2048]{1,0:T(8,128)(2,1)} fusion(bf16[3,2048,512]{2,1,0:T(8,128)(2,1)} %param.16, bf16[1,1024,512]{2,1,0:T(8,128)(2,1)S(1)} %copy.56, bf16[1,1024,512]{2,1,0:T(8,128)(2,1)S(1)} %copy.55, bf16[1,1024,512]{2,1,0:T(8,128)(2,1)S(1)} %copy.54), kind=kOutput, calls=%fused_computation.56 | convolution fusion | flops 6447693824 | bytes 13631488 | tf_op jit(solution)/shard_map/kte,kde->td/dot_general | solution.py:243
  643.1 11.9 %convert_bitcast_fusion.1 = bf16[3,2048,512]{1,2,0:T(8,128)(2,1)} fusion(f32[2048]{0:T(1024)S(1)} %bitcast.209, f32[2048]{0:T(1024)S(1)} %bitcast.195, bf16[1,1024,512]{2,1,0:T(8,128)(2,1)S(1)} %copy.56, bf16[1,1024,512]{2,1,0:T(8,128)(2,1)S(1)} %copy.55, bf16[1,1024,512]{2,1,0:T(8,128)(2,1)S(1)} %copy.54, bf16[1024,2048]{1,0:T(8,128)(2,1)} %param.14, ...), kind=kOutput, calls=%fused_computation.67 | convolution fusion | flops 6461325312 | bytes 13656064 | tf_op jit(solution)/shard_map/td,kte->kde/dot_general | solution.py:240
  655.7 19.2 %convert_bitcast_fusion = bf16[2,2048,1408]{1,2,0:T(8,128)(2,1)} fusion(bf16[1,1024,1408]{2,1,0:T(8,128)(2,1)} %copy-done.34, bf16[1,1024,1408]{2,1,0:T(8,128)(2,1)} %copy-done.33, f32[1024,2048]{1,0:T(8,128)} %copy-done.9, f32[2048]{0:T(1024)S(1)} %bitcast.207, f32[2048]{0:T(1024)S(1)} %bitcast.201), kind=kOutput, calls=%fused_computation.52 | convolution fusion | flops 11826102272 | bytes 25706496 | tf_op jit(solution)/shard_map/td,ktf->kdf/dot_general | solution.py:205
  675.0 3.1 fusion.52
  683.1 42.1 %reduce-scatter.14.cloned.1.call-done = bf16[1408,256]{1,0:T(8,128)(2,1)} async-done(((bf16[1408,2048]{1,0:T(8,128)(2,1)}), bf16[1408,256]{1,0:T(8,128)(2,1)}) %reduce-scatter.14.cloned.1.call-update) | async-done | bytes 720912 | tf_op jit(solution)/shard_map/reduce_scatter | solution.py:275
  727.5 44.6 %reduce-scatter.6.cloned.1.call-done = bf16[256,2048]{1,0:T(8,128)(2,1)} async-done(((bf16[1024,2048]{1,0:T(8,128)(2,1)}), bf16[256,2048]{1,0:T(8,128)(2,1)}) %reduce-scatter.6.cloned.1.call-update) | async-done | bytes 1048592 | tf_op jit(solution)/shard_map/reduce_scatter | solution.py:242
  774.8 44.0 %all-reduce = (f32[3,2048]{1,0:T(4,128)}, f32[2,2048]{1,0:T(2,128)}, f32[2,2048]{1,0:T(2,128)}) all-reduce(f32[3,2048]{1,0:T(4,128)S(1)} %constant_dynamic-update-slice_fusion, f32[2,2048]{1,0:T(2,128)S(1)} %pad_maximum_fusion.7, f32[2,2048]{1,0:T(2,128)S(1)} %pad_maximum_fusion.8), channel_id=1, replica_groups=mesh['dp'=8,'tensor'=4] {'dp','tensor'}, use_global_device_ids=true, to_apply=%region_24.25 | all-reduce | flops 14336 | bytes 114688 | tf_op jit(solution)/shard_map/psum | solution.py:261
  818.9 4.6 fusion.49
  823.5 71.7 %reduce-scatter.8.cloned.1.call-done = bf16[3,256,512]{1,2,0:T(8,128)(2,1)} async-done(((bf16[3,2048,512]{1,2,0:T(8,128)(2,1)}), bf16[3,256,512]{1,2,0:T(8,128)(2,1)}) %reduce-scatter.8.cloned.1.call-update) | async-done | bytes 786448 | tf_op jit(solution)/shard_map/reduce_scatter | solution.py:266
  897.7 193.1 %reduce-scatter.12.cloned.1.call-done = bf16[2,256,1408]{1,2,0:T(8,128)(2,1)} async-done(((bf16[2,2048,1408]{1,2,0:T(8,128)(2,1)}), bf16[2,256,1408]{1,2,0:T(8,128)(2,1)}) %reduce-scatter.12.cloned.1.call-update) | async-done | bytes 1441808 | tf_op jit(solution)/shard_map/reduce_scatter | solution.py:272
  1090.8 3.0 copy.60
  (169 shorter events, 67.4 us)
Async XLA Ops:
  7.2 62.1 %copy-start = (bf16[512,2048]{1,0:T(8,128)(2,1)S(1)}, bf16[512,2048]{1,0:T(8,128)(2,1)}, u32[]{:S(2)}) copy-start(bf16[512,2048]{1,0:T(8,128)(2,1)} %param.18) | copy-start | bytes 6291460
  7.2 4.9 copy-start.31
  7.2 5.0 copy-start.25
  7.2 223.5 %all-reduce.5.cloned.1.call-start = ((), (), s32[]{:S(2)}) async-start(), calls=%async_computation.5 | async-start | bytes 16777216 | tf_op jit(solution)/shard_map/psum | solution.py:181
  7.3 3.6 copy-start.8
  7.3 5.5 copy-start.26
  10.9 13.0 %copy-start.19 = (f32[1024]{0:T(1024)}, f32[1024]{0:T(1024)S(1)}, u32[]{:S(2)}) copy-start(f32[1024]{0:T(1024)S(1)} %broadcast_multiply_fusion.3) | copy-start | bytes 12292
  12.1 11.7 %copy-start.22 = (f32[1024]{0:T(1024)}, f32[1024]{0:T(1024)S(1)}, u32[]{:S(2)}) copy-start(f32[1024]{0:T(1024)S(1)} %add_rsqrt_fusion.1) | copy-start | bytes 12292
  12.8 11.1 %copy-start.15 = (f32[1,2048]{1,0:T(1,128)}, f32[1,2048]{1,0:T(1,128)S(1)}, u32[]{:S(2)}) copy-start(f32[1,2048]{1,0:T(1,128)S(1)} %get-tuple-element.344) | copy-start | bytes 24580
  13.4 10.5 copy-start.29
  23.9 3.5 copy-start.32
  31.5 3.6 copy-start.12
  74.9 155.8 %copy-start.20 = (f32[1024]{0:T(1024)S(1)}, f32[1024]{0:T(1024)}, u32[]{:S(2)}) copy-start(f32[1024]{0:T(1024)} %copy-done.19) | copy-start | bytes 12292
  74.9 155.8 %copy-start.23 = (f32[1024]{0:T(1024)S(1)}, f32[1024]{0:T(1024)}, u32[]{:S(2)}) copy-start(f32[1024]{0:T(1024)} %copy-done.22) | copy-start | bytes 12292
  75.0 376.6 %all-reduce.9.cloned.1.call-start = ((), (), s32[]{:S(2)}) async-start(), calls=%async_computation.7 | async-start | bytes 16777216 | tf_op jit(solution)/shard_map/psum | solution.py:208
  238.4 3.2 copy-start.3
  241.6 4.0 copy-start.17
  241.6 4.0 copy-start.27
  242.4 3.2 copy-start.9
  278.6 1.6 copy-start.33
  278.6 2.5 copy-start.34
  298.4 376.6 %all-reduce.7.cloned.1.call-start = ((), (), s32[]{:S(2)}) async-start(), calls=%async_computation.6 | async-start | bytes 8388608 | tf_op jit(solution)/shard_map/psum | solution.py:193
  309.4 371.9 %reduce-scatter.10.cloned.1.call-start = ((), (), s32[]{:S(2)}) async-start(), calls=%async_computation.10 | async-start | bytes 2359296 | tf_op jit(solution)/shard_map/reduce_scatter | solution.py:269
  451.6 8.5 copy-start.6
  451.6 10.2 copy-start.11
  467.1 3.2 copy-start.10
  474.0 251.2 %reduce-scatter.14.cloned.1.call-start = ((), (), s32[]{:S(2)}) async-start(), calls=%async_computation.12 | async-start | bytes 6488064 | tf_op jit(solution)/shard_map/reduce_scatter | solution.py:275
  484.8 287.3 %reduce-scatter.6.cloned.1.call-start = ((), (), s32[]{:S(2)}) async-start(), calls=%async_computation.8 | async-start | bytes 5242880 | tf_op jit(solution)/shard_map/reduce_scatter | solution.py:242
  509.3 9.6 copy-start.7
  518.9 9.0 copy-start.2
  527.9 4.0 copy-start.4
  534.8 20.6 %copy-start.5 = (f32[1024,8,64]{0,2,1:T(8,128)}, f32[1024,8,64]{0,2,1:T(8,128)S(1)}, u32[]{:S(2)}) copy-start(f32[1024,8,64]{0,2,1:T(8,128)S(1)} %bitcast_add_fusion.4) | copy-start | bytes 6291460 | tf_op jit(solution)/shard_map/while
  570.9 9.5 copy-start.7
  580.4 9.6 copy-start.2
  590.0 4.0 copy-start.4
  596.9 20.6 %copy-start.5 = (f32[1024,8,64]{0,2,1:T(8,128)}, f32[1024,8,64]{0,2,1:T(8,128)S(1)}, u32[]{:S(2)}) copy-start(f32[1024,8,64]{0,2,1:T(8,128)S(1)} %bitcast_add_fusion.4) | copy-start | bytes 6291460 | tf_op jit(solution)/shard_map/while
  617.6 6.4 copy-start.13
  617.6 6.4 copy-start.14
  631.9 11.2 %copy-start.16 = (f32[1,2048]{1,0:T(1,128)S(1)}, f32[1,2048]{1,0:T(1,128)}, u32[]{:S(2)}) copy-start(f32[1,2048]{1,0:T(1,128)} %copy-done.15) | copy-start | bytes 24580
  631.9 11.2 %copy-start.21 = (f32[1024]{0:T(1024)S(1)}, f32[1024]{0:T(1024)}, u32[]{:S(2)}) copy-start(f32[1024]{0:T(1024)} %copy-done.19) | copy-start | bytes 12292
  631.9 11.2 %copy-start.24 = (f32[1024]{0:T(1024)S(1)}, f32[1024]{0:T(1024)}, u32[]{:S(2)}) copy-start(f32[1024]{0:T(1024)} %copy-done.22) | copy-start | bytes 12292
  631.9 11.2 %copy-start.30 = (f32[1,2048]{1,0:T(1,128)S(1)}, f32[1,2048]{1,0:T(1,128)}, u32[]{:S(2)}) copy-start(f32[1,2048]{1,0:T(1,128)} %copy-done.29) | copy-start | bytes 24580
  643.0 252.1 %reduce-scatter.8.cloned.1.call-start = ((), (), s32[]{:S(2)}) async-start(), calls=%async_computation.9 | async-start | bytes 7077888 | tf_op jit(solution)/shard_map/reduce_scatter | solution.py:266
  655.0 0.7 copy-start.18
  655.0 0.7 copy-start.28
  655.0 435.8 %reduce-scatter.12.cloned.1.call-start = ((), (), s32[]{:S(2)}) async-start(), calls=%async_computation.11 | async-start | bytes 12976128 | tf_op jit(solution)/shard_map/reduce_scatter | solution.py:272
  818.9 274.9 %copy-start.1 = (bf16[512,2048]{1,0:T(8,128)(2,1)S(1)}, bf16[512,2048]{1,0:T(8,128)(2,1)}, u32[]{:S(2)}) copy-start(bf16[512,2048]{1,0:T(8,128)(2,1)} %param.18) | copy-start | bytes 6291460
Sparse Core Ops, SparseCore 0:
  75.1 155.5 all-reduce.4
  298.5 153.0 all-reduce.8
  454.0 85.6 all-reduce.6
  543.4 68.3 reduce-scatter.9
  615.8 109.3 reduce-scatter.13
  727.7 44.2 reduce-scatter.5
  775.7 119.4 reduce-scatter.7
  898.7 192.0 reduce-scatter.11
where the time goes:
time: 1110 us; the launch traced here: 1100 us
  waiting for transfers between devices  649 us (58%)
  matrix products  223 us (20%)
  local copies, waits for them, and re-layouts  86 us (8%)
  other arithmetic  82.6 us (7%)
  blocking collectives  44 us (4%)
  between operations  14.9 us (1%)
    reduce_scatter x1, waiting for transfers between devices, body(): lax.psum_scatter(gate_up_grad.astype(jnp.bfloat16), 'dp', scatter_dimensi...  193 us
    psum x1, waiting for transfers between devices, body(): lax.psum(jnp.dot(heads_out, out_weight, preferred_element_type=jnp.float3...  156 us
    psum x1, waiting for transfers between devices, body(): lax.psum(jnp.einsum('ktf,kdf->td', gate_up_low, gate_up_weight, preferred...  142 us
    reduce_scatter x1, waiting for transfers between devices, body(): lax.psum_scatter(qkv_grad.astype(jnp.bfloat16), 'dp', scatter_dimension=1...  71.7 us
    reduce_scatter x1, waiting for transfers between devices, body(): lax.psum_scatter(jnp.einsum('kte,kde->td', projected_low, qkv_weight, pre...  44.6 us
    psum x1, blocking collectives, body(): lax.psum((jnp.stack([gain_first, gain_second]), jnp.stack([shift_first, s...  44 us
    reduce_scatter x1, waiting for transfers between devices, body(): lax.psum_scatter(down_grad.astype(jnp.bfloat16), 'dp', scatter_dimension=...  42.1 us
    dynamic_update_slice x4, local copies, waits for them, and re-layouts, attend_backward(): lax.scan(one_block, (zeros_kv, zeros_kv), (queries.reshape(blocks, block_...  41.2 us
  transfers between devices with their start and end apart: 8, of which 6 were waited for; matrix products, arithmetic and copies ran while one was open for 22% of the time, Pallas kernels for 0%

commit v1 on v0

v1 whole, which is shorter than its diff:
```python
import functools

import jax
import jax.numpy as jnp
from jax import lax
from jax.experimental import pallas as pl
from jax.experimental.pallas import tpu as pltpu
from jax.sharding import PartitionSpec as P

HD = 64
SEQ_MAX = 512
BQ = 256
F32 = jnp.float32
BF16 = jnp.bfloat16
LOG2E = 1.4426950408889634
VMEM_LIMIT = 60 * 1024 * 1024


def norm_parts(values):
    centred = values - jnp.mean(values, axis=-1, keepdims=True)
    inverse = lax.rsqrt(jnp.mean(centred * centred, axis=-1, keepdims=True) + 1e-05)
    return (centred * inverse, inverse)


def norm_back(unit, inverse, gain_row, grad_rows):
    scaled = grad_rows * gain_row
    return inverse * (
        scaled
        - jnp.mean(scaled, axis=-1, keepdims=True)
        - unit * jnp.mean(scaled * unit, axis=-1, keepdims=True)
    )


def positions(lengths, row_count):
    indices = jnp.arange(row_count, dtype=jnp.int32)
    count = lengths.shape[0]
    order = jnp.arange(count, dtype=jnp.int32)
    ends_at = jnp.sum(jnp.where(order[:, None] <= order[None, :], lengths[:, None], 0), axis=0)
    passed = indices[:, None] >= ends_at[None, :]
    begins = jnp.sum(jnp.where(passed, lengths[None, :], 0), axis=1, dtype=jnp.int32)
    places = (indices - begins).astype(F32)
    half = HD // 8
    lane = jnp.arange(128, dtype=jnp.int32) % HD
    rates = 10000.0 ** (-((lane % half).astype(F32) / half))
    angles = places[:, None] * rates[None, :]
    cosine, sine = jnp.cos(angles), jnp.sin(angles)
    turn = jnp.where(lane < 2 * half, cosine, 1.0)
    ahead = jnp.where(lane < half, -sine, 0.0)
    behind = jnp.where((lane >= half) & (lane < 2 * half), sine, 0.0)
    return begins, turn, ahead, behind


def turned(values, turn, ahead, behind):
    half = HD // 8
    width = values.shape[1]
    times = width // turn.shape[1]

    def wide(table):
        return jnp.concatenate([table] * times, axis=1) if times > 1 else table

    return (
        values * wide(turn)
        + pltpu.roll(values, width - half, 1) * wide(ahead)
        + pltpu.roll(values, half, 1) * wide(behind)
    )


def qkv_kernel(x_ref, w_ref, b_ref, g_ref, s_ref, c_ref, a_ref, h_ref, n_ref, q_ref, k_ref, v_ref):
    unit, _ = norm_parts(x_ref[...].astype(F32))
    normed = (unit * g_ref[...] + s_ref[...]).astype(BF16)
    n_ref[...] = normed
    for j, out in enumerate((q_ref, k_ref, v_ref)):
        got = jnp.dot(normed, w_ref[j], preferred_element_type=F32) + b_ref[j : j + 1, :]
        if j < 2:
            got = turned(got, c_ref[...], a_ref[...], h_ref[...])
        out[...] = got.astype(BF16)


def project(tokens, weight, bias, gain, shift, tables):
    rows, full = tokens.shape
    width = weight.shape[2]
    block = min(256, rows)

    def whole(*dims):
        return pl.BlockSpec(dims, lambda i: (0,) * len(dims))

    def by_row(columns):
        return pl.BlockSpec((block, columns), lambda i: (i, 0))

    return pl.pallas_call(
        qkv_kernel,
        grid=(rows // block,),
        in_specs=[
            by_row(full),
            whole(3, full, width),
            whole(3, width),
            whole(1, full),
            whole(1, full),
            by_row(128),
            by_row(128),
            by_row(128),
        ],
        out_specs=[by_row(full), by_row(width), by_row(width), by_row(width)],
        out_shape=[jax.ShapeDtypeStruct((rows, full), BF16)]
        + [jax.ShapeDtypeStruct((rows, width), BF16)] * 3,
        compiler_params=pltpu.CompilerParams(vmem_limit_bytes=VMEM_LIMIT),
        cost_estimate=pl.CostEstimate(
            flops=6 * rows * full * width,
            bytes_accessed=2 * (2 * rows * full + 3 * full * width + 3 * rows * width),
            transcendentals=0,
        ),
    )(tokens, weight, bias.astype(F32), gain[None], shift[None], *tables)


def spans(step, blocks):
    most = SEQ_MAX // BQ + 1
    forms = []
    for at in range(min(most - 1, blocks)):
        forms.append((step == at, 0, (at + 1) * BQ))
    if blocks >= most:
        first = pl.multiple_of((step - (most - 1)) * BQ, BQ)
        forms.append((step >= most - 1, first, most * BQ))
    return forms


def allowed_bias(begin_row, first, count, step):
    key_at = first + lax.broadcasted_iota(jnp.int32, (count, BQ), 0)
    query_at = step * BQ + lax.broadcasted_iota(jnp.int32, (count, BQ), 1)
    return jnp.where((key_at >= begin_row) & (key_at <= query_at), 0.0, -1e30)


def over_rows(left, right):
    return lax.dot_general(left, right, (((0,), (0,)), ((), ())), preferred_element_type=F32)


def over_columns(left, right):
    return lax.dot_general(left, right, (((1,), (1,)), ((), ())), preferred_element_type=F32)


def attend_kernel(blocks, begin_ref, q_ref, k_ref, v_ref, o_ref, l_ref):
    step = pl.program_id(1)
    factor = HD**-0.5 * LOG2E

    def one(first, count):
        bias = allowed_bias(begin_ref[...], first, count, step)
        rows = pl.ds(first, count)
        parts = []
        for head in range(2):
            lanes = slice(head * HD, (head + 1) * HD)
            scores = over_columns(k_ref[rows, lanes], q_ref[:, lanes]) * factor + bias
            top = jnp.max(scores, axis=0, keepdims=True)
            probs = jnp.exp2(scores - top)
            total = jnp.sum(probs, axis=0, keepdims=True)
            got = over_rows(v_ref[rows, lanes], probs.astype(BF16))
            parts.append(got * (1.0 / total))
            l_ref[head] = top + jnp.log2(total)
        o_ref[...] = jnp.concatenate(parts, axis=0).T.astype(BF16)

    for condition, first, count in spans(step, blocks):
        pl.when(condition)(functools.partial(one, first, count))


def attend(begins, queries, keys, values):
    rows, width = queries.shape
    blocks = rows // BQ
    return pl.pallas_call(
        functools.partial(attend_kernel, blocks),
        grid=(width // 128, blocks),
        in_specs=[
            pl.BlockSpec((1, BQ), lambda h, i: (0, i)),
            pl.BlockSpec((BQ, 128), lambda h, i: (i, h)),
            pl.BlockSpec((rows, 128), lambda h, i: (0, h)),
            pl.BlockSpec((rows, 128), lambda h, i: (0, h)),
        ],
        out_specs=[
            pl.BlockSpec((BQ, 128), lambda h, i: (i, h)),
            pl.BlockSpec((2, 1, BQ), lambda h, i: (h, 0, i)),
        ],
        out_shape=[
            jax.ShapeDtypeStruct((rows, width), BF16),
            jax.ShapeDtypeStruct((width // HD, 1, rows), F32),
        ],
        compiler_params=pltpu.CompilerParams(vmem_limit_bytes=VMEM_LIMIT),
        cost_estimate=pl.CostEstimate(
            flops=8 * rows * 768 * width, bytes_accessed=8 * rows * width, transcendentals=rows * 768 * width // HD
        ),
    )(begins[None], queries, keys, values)


def attend_back_kernel(
    blocks, begin_ref, q_ref, k_ref, v_ref, g_ref, l_ref, cq_ref, aq_ref, hq_ref, c_ref, a_ref, h_ref,
    dq_ref, dk_ref, dv_ref, sum_k, sum_v,
):
    step = pl.program_id(1)
    scale = HD**-0.5
    factor = scale * LOG2E

    @pl.when(step == 0)
    def _():
        sum_k[...] = jnp.zeros_like(sum_k)
        sum_v[...] = jnp.zeros_like(sum_v)

    def one(first, count):
        bias = allowed_bias(begin_ref[...], first, count, step)
        rows = pl.ds(first, count)
        dq, dk, dv = [], [], []
        for head in range(2):
            lanes = slice(head * HD, (head + 1) * HD)
            query, key, value, grad = q_ref[:, lanes], k_ref[rows, lanes], v_ref[rows, lanes], g_ref[:, lanes]
            probs = jnp.exp2(over_columns(key, query) * factor + bias - l_ref[head])
            weighed = probs * over_columns(value, grad)
            inner = jnp.sum(weighed, axis=0, keepdims=True)
            score_grad = (weighed - probs * inner).astype(BF16)
            dv.append(jnp.dot(probs.astype(BF16), grad, preferred_element_type=F32))
            dk.append(jnp.dot(score_grad, query, preferred_element_type=F32))
            dq.append(over_rows(key, score_grad))
        sum_k[rows, :] += jnp.concatenate(dk, axis=1)
        sum_v[rows, :] += jnp.concatenate(dv, axis=1)
        query_grad = jnp.concatenate(dq, axis=0).T * scale
        dq_ref[...] = turned(query_grad, cq_ref[...], -aq_ref[...], -hq_ref[...]).astype(BF16)

    for condition, first, count in spans(step, blocks):
        pl.when(condition)(functools.partial(one, first, count))

    @pl.when(step == blocks - 1)
    def _():
        dk_ref[...] = turned(sum_k[...] * scale, c_ref[...], -a_ref[...], -h_ref[...]).astype(BF16)
        dv_ref[...] = sum_v[...].astype(BF16)


def attend_back(begins, queries, keys, values, grads, logs, tables):
    rows, width = queries.shape
    blocks = rows // BQ
    part = pl.BlockSpec((BQ, 128), lambda h, i: (i, h))
    column = pl.BlockSpec((rows, 128), lambda h, i: (0, h))
    return pl.pallas_call(
        functools.partial(attend_back_kernel, blocks),
        grid=(width // 128, blocks),
        in_specs=[
            pl.BlockSpec((1, BQ), lambda h, i: (0, i)),
            part,
            column,
            column,
            part,
            pl.BlockSpec((2, 1, BQ), lambda h, i: (h, 0, i)),
        ]
        + [pl.BlockSpec((BQ, 128), lambda h, i: (i, 0))] * 3
        + [pl.BlockSpec((rows, 128), lambda h, i: (0, 0))] * 3,
        out_specs=[part, column, column],
        out_shape=[jax.ShapeDtypeStruct((rows, width), BF16)] * 3,
        scratch_shapes=[pltpu.VMEM((rows, 128), F32)] * 2,
        compiler_params=pltpu.CompilerParams(vmem_limit_bytes=VMEM_LIMIT),
        cost_estimate=pl.CostEstimate(
            flops=20 * rows * 768 * width, bytes_accessed=16 * rows * width, transcendentals=rows * 768 * width // HD
        ),
    )(begins[None], queries, keys, values, grads, logs, *tables, *tables)


def dot(left, right):
    return jnp.dot(left, right, preferred_element_type=F32)


def pick(values, at, axis):
    return lax.dynamic_index_in_dim(values, at, axis, keepdims=False)


def swap(values, axis, bit):
    size = lax.axis_size(axis)
    return lax.ppermute(values, axis, [(i, i ^ (1 << bit)) for i in range(size)])


def sum_rows(left, times):
    size = lax.axis_size("tensor")
    me = lax.axis_index("tensor")
    bits = size.bit_length() - 1
    rows = left.shape[0] // size
    core = me & 1
    by_core = left.reshape(size // 2, 2, rows, left.shape[1])

    def product(of):
        taken = pick(by_core, of, 1)
        got = times(taken.reshape(-1, left.shape[1]))
        return got.reshape(size // 2, rows, got.shape[-1])

    arrived = swap(product(1 - core).astype(BF16), "tensor", 0)
    total = product(core) + arrived.astype(F32)
    for bit in range(1, bits):
        mine = (me >> bit) & 1
        total = total.reshape(-1, 2, *total.shape[1:])
        arrived = swap(pick(total, 1 - mine, 1).astype(BF16), "tensor", bit)
        total = pick(total, mine, 1) + arrived.astype(F32)
    return total[0]


def spread_rows(own):
    size = lax.axis_size("tensor")
    me = lax.axis_index("tensor")
    bits = size.bit_length() - 1
    rows, columns = own.shape
    held = own[None]
    for bit in reversed(range(bits)):
        other = swap(held, "tensor", bit)
        mine = ((me >> bit) & 1) == 0
        held = jnp.stack([jnp.where(mine, held, other), jnp.where(mine, other, held)], axis=1)
        held = held.reshape(-1, rows, columns)
    return held.reshape(-1, columns)


def sum_parts(send, keep, shape_back):
    size = lax.axis_size("dp")
    me = lax.axis_index("dp")
    bits = size.bit_length() - 1
    arrived = swap(send, "dp", 0)
    total = keep + arrived.astype(F32)
    for bit in range(1, bits):
        mine = (me >> bit) & 1
        total = total.reshape(-1, 2, *total.shape[1:])
        arrived = swap(pick(total, 1 - mine, 1).astype(BF16), "dp", bit)
        total = pick(total, mine, 1) + arrived.astype(F32)
    return total[0]


def halves(values):
    size = lax.axis_size("dp")
    me = lax.axis_index("dp") & 1
    cut = values.reshape(values.shape[0], size // 2, 2, values.shape[1] // size)
    return pick(cut, 1 - me, 2), pick(cut, me, 2)


def body(
    tokens,
    seq_lengths,
    qkv_weight,
    qkv_bias,
    out_weight,
    gate_up_weight,
    down_weight,
    norm_gains,
    norm_shifts,
    cotangent,
):
    row_count, full_width = tokens.shape
    share = row_count // lax.axis_size("tensor")
    first_row = lax.axis_index("tensor") * share
    local_width = qkv_weight.shape[2]

    def own_rows(values):
        return lax.dynamic_slice_in_dim(values, first_row, share, 0)

    begins, *tables = positions(seq_lengths[0], row_count)
    normed, queries, keys, values = project(
        tokens, qkv_weight, qkv_bias, norm_gains[0], norm_shifts[0], tables
    )
    heads_out, logs = attend(begins, queries, keys, values)
    inputs_own = own_rows(tokens).astype(F32)
    cotangent_own = own_rows(cotangent).astype(F32)
    residual_own = inputs_own + sum_rows(heads_out, lambda left: dot(left, out_weight))
    unit_second, inverse_second = norm_parts(residual_own)
    second = spread_rows((unit_second * norm_gains[1] + norm_shifts[1]).astype(BF16))
    gate = dot(second, gate_up_weight[0])
    upper = dot(second, gate_up_weight[1])
    hidden_grad = jnp.einsum("td,fd->tf", cotangent, down_weight, preferred_element_type=F32)
    sigmoid_gate = jax.nn.sigmoid(gate)
    activated = gate * sigmoid_gate
    hidden = (activated * upper).astype(BF16)
    gate_grad = (
        hidden_grad * upper * (sigmoid_gate * (1.0 + gate * (1.0 - sigmoid_gate)))
    ).astype(BF16)
    upper_grad = (hidden_grad * activated).astype(BF16)

    cotangent_send, cotangent_keep = halves(cotangent)
    down_part = sum_parts(
        jnp.einsum("tf,tbc->bfc", hidden, cotangent_send, preferred_element_type=F32).astype(BF16),
        jnp.einsum("tf,tbc->bfc", hidden, cotangent_keep, preferred_element_type=F32),
        None,
    )
    second_send, second_keep = halves(second)

    def weight_part(send, keep, grads):
        return sum_parts(
            jnp.einsum("tbd,tf->bdf", send, grads, preferred_element_type=F32).astype(BF16),
            jnp.einsum("tbd,tf->bdf", keep, grads, preferred_element_type=F32),
            None,
        )

    gate_up_part = jnp.stack(
        [
            weight_part(second_send, second_keep, gate_grad),
            weight_part(second_send, second_keep, upper_grad),
        ]
    )
    branch_own = sum_rows(hidden, lambda left: dot(left, down_weight))
    block_out = (residual_own + branch_own).astype(BF16)

    def second_back(left):
        gates, uppers = jnp.split(left, 2, axis=1)
        return jnp.einsum(
            "tf,df->td", gates, gate_up_weight[0], preferred_element_type=F32
        ) + jnp.einsum("tf,df->td", uppers, gate_up_weight[1], preferred_element_type=F32)

    second_grad_own = sum_rows(jnp.concatenate([gate_grad, upper_grad], axis=1), second_back)
    residual_grad_own = cotangent_own + norm_back(
        unit_second, inverse_second, norm_gains[1], second_grad_own
    )
    residual_low = spread_rows(residual_grad_own.astype(BF16))
    gain_second = jnp.sum(second_grad_own * unit_second, axis=0)
    shift_second = jnp.sum(second_grad_own, axis=0)
    heads_grad = jnp.einsum(
        "td,ed->te", residual_low, out_weight, preferred_element_type=F32
    ).astype(BF16)
    low_send, low_keep = halves(residual_low)
    out_part = sum_parts(
        jnp.einsum("tf,tbc->bfc", heads_out, low_send, preferred_element_type=F32).astype(BF16),
        jnp.einsum("tf,tbc->bfc", heads_out, low_keep, preferred_element_type=F32),
        None,
    )
    projected_low = attend_back(begins, queries, keys, values, heads_grad, logs, tables)
    normed_send, normed_keep = halves(normed)
    qkv_part = jnp.stack([weight_part(normed_send, normed_keep, g) for g in projected_low])
    bias_local = jnp.stack([jnp.sum(g, axis=0, dtype=F32) for g in projected_low])

    def normed_back(left):
        return sum(
            jnp.einsum("te,de->td", piece, qkv_weight[j], preferred_element_type=F32)
            for j, piece in enumerate(jnp.split(left, 3, axis=1))
        )

    normed_grad_own = sum_rows(jnp.concatenate(projected_low, axis=1), normed_back)
    unit_first, inverse_first = norm_parts(inputs_own)
    input_grad = residual_grad_own + norm_back(
        unit_first, inverse_first, norm_gains[0], normed_grad_own
    )
    gain_first = jnp.sum(normed_grad_own * unit_first, axis=0)
    shift_first = jnp.sum(normed_grad_own, axis=0)
    bias_placed = lax.dynamic_update_slice(
        jnp.zeros((3, full_width), F32),
        bias_local,
        (0, lax.axis_index("tensor") * local_width),
    )
    gains_grad, shifts_grad, bias_grad = lax.psum(
        (jnp.stack([gain_first, gain_second]), jnp.stack([shift_first, shift_second]), bias_placed),
        ("dp", "tensor"),
    )
    return (
        block_out,
        input_grad,
        qkv_part,
        bias_grad,
        out_part,
        gate_up_part,
        down_part,
        gains_grad,
        shifts_grad,
    )


def solution(mesh):
    return jax.shard_map(
        body,
        mesh=mesh,
        in_specs=(
            P("dp", None),
            P("dp", None),
            P(None, None, "tensor"),
            P(None, "tensor"),
            P("tensor", None),
            P(None, None, "tensor"),
            P("tensor", None),
            P(),
            P(),
            P("dp", None),
        ),
        out_specs=(
            P(("dp", "tensor"), None),
            P(("dp", "tensor"), None),
            P(None, "dp", "tensor"),
            P(),
            P("tensor", "dp"),
            P(None, "dp", "tensor"),
            P("tensor", "dp"),
            P(),
            P(),
        ),
        check_vma=False,
    )
```

time: 1110 us -> 859 us (0.77)
  waiting for transfers between devices: 649 us -> 300 us
  local copies, waits for them, and re-layouts: 86 us -> 192 us
  Pallas kernels: 0 us -> 62.4 us
  matrix products: 223 us -> 165 us
  starting transfers between devices: 0.33 us -> 36 us
  other arithmetic: 82.6 us -> 47.3 us
  between operations: 14.9 us -> 2.05 us
    reduce_scatter x5 -> x0, waiting for transfers between devices: 351 us -> none  [the longest x1 193 us: body(): lax.psum_scatter(gate_up_grad.astype(jnp.bfloat16), 'dp', scatter_dimensi...]
    ppermute x0 -> x33, waiting for transfers between devices: none -> 300 us  [swap(): return lax.ppermute(values, axis, [(i, i ^ 1 << bit) for i in range(size)])]
    psum x3 -> x0, waiting for transfers between devices: 298 us -> none  [the longest x1 156 us: body(): lax.psum(jnp.dot(heads_out, out_weight, preferred_element_type=jnp.float3...]
    dynamic_slice x4 -> x18, local copies, waits for them, and re-layouts: 0.04 us -> 116 us  [pick(): return lax.dynamic_index_in_dim(values, at, axis, keepdims=False)]
    pallas_call x0 -> x3, Pallas kernels: none -> 62.4 us  [the longest x1 28.4 us: attend_back(): pl.pallas_call(functools.partial(attend_back_kernel, blocks), grid=(width...]
    dot_general x25 -> x31, matrix products: 217 us -> 160 us  [the longest x6 46.2 us: dot(): return jnp.dot(left, right, preferred_element_type=F32)]
    dynamic_update_slice x5 -> x0, local copies, waits for them, and re-layouts: 41.2 us -> none  [the longest x4 41.2 us: attend_backward(): lax.scan(one_block, (zeros_kv, zeros_kv), (queries.reshape(blocks, block_...]
    ppermute x0 -> x33, starting transfers between devices: none -> 36 us  [swap(): return lax.ppermute(values, axis, [(i, i ^ 1 << bit) for i in range(size)])]
  transfers between devices with their start and end apart: 8 -> 33, of which waited for: 6 -> 15; matrix products, arithmetic and copies ran while one was open for 22% -> 26% of each run, Pallas kernels for 0% -> 0%
where the time goes in v1:
time: 859 us; the launch traced here: 847 us
  waiting for transfers between devices  300 us (35%)
  local copies, waits for them, and re-layouts  192 us (22%)
  matrix products  165 us (19%)
  Pallas kernels  62.4 us (7%)
  other arithmetic  47.3 us (6%)
  blocking collectives  41.7 us (5%)
  starting transfers between devices  36 us (4%)
    ppermute x33, waiting for transfers between devices, swap(): return lax.ppermute(values, axis, [(i, i ^ 1 << bit) for i in range(size)])  300 us
    dynamic_slice x18, local copies, waits for them, and re-layouts, pick(): return lax.dynamic_index_in_dim(values, at, axis, keepdims=False)  116 us
    dot_general x6, matrix products, dot(): return jnp.dot(left, right, preferred_element_type=F32)  46.2 us
    psum x1, blocking collectives, body(): lax.psum((jnp.stack([gain_first, gain_second]), jnp.stack([shift_first, s...  41.7 us
    ppermute x33, starting transfers between devices, swap(): return lax.ppermute(values, axis, [(i, i ^ 1 << bit) for i in range(size)])  36 us
    unnamed x112, local copies, waits for them, and re-layouts  35.8 us
    pallas_call x1, Pallas kernels, attend_back(): pl.pallas_call(functools.partial(attend_back_kernel, blocks), grid=(width...  28.4 us
    dot_general x6, matrix products, normed_back(): jnp.einsum('te,de->td', piece, qkv_weight[j], preferred_element_type=F32)  28.2 us
  transfers between devices with their start and end apart: 33, of which 15 were waited for; matrix products, arithmetic and copies ran while one was open for 26% of the time, Pallas kernels for 0%

profile of v1, /device:TPU:0, one launch (start us, length us, event | category | flops | bytes accessed | tf_op | source)
XLA Modules:
  0.0 847.2 jit_solution(8438828988410369533)
XLA Ops:
  8.2 13.9 %shard_map.169 = (bf16[1024,2048]{1,0:T(8,128)(2,1)}, bf16[1024,512]{1,0:T(8,128)(2,1)}, bf16[1024,512]{1,0:T(8,128)(2,1)}, bf16[1024,512]{1,0:T(8,128)(2,1)}) custom-call(bf16[1024,2048]{1,0:T(8,128)(2,1)} %x_ref.1, bf16[3,2048,512]{2,1,0:T(8,128)(2,1)} %w_ref.1, f32[3,512]{1,0:T(4,128)} %convert_element_type.283.b_ref, f32[1,2048]{1,0:T(1,128)} %get-tuple-element.70.g_ref, ...), custom_call_target="tpu_custom_call" | custom-call | flops 6442450944 | bytes 17825792 | tf_op jit(solution)/shard_map/pallas_call | solution.py:90
  22.1 20.2 %shard_map.170 = (bf16[1024,512]{1,0:T(8,128)(2,1)}, f32[8,1,1024]{2,1,0:T(1,128)}) custom-call(s32[1,1024]{1,0:T(1,128)} %bitcast.384, bf16[1024,512]{1,0:T(8,128)(2,1)} %get-tuple-element.18.q_ref, bf16[1024,512]{1,0:T(8,128)(2,1)} %get-tuple-element.19.k_ref, bf16[1024,512]{1,0:T(8,128)(2,1)} %get-tuple-element.20.v_ref), custom_call_target="tpu_custom_call" | custom-call | flops 3221225472 | bytes 4194304 | tf_op jit(solution)/shard_map/pallas_call | solution.py:166
  58.6 7.8 reshape.285
  67.9 14.3 %collective-permute-done.1 = bf16[1,256,2048]{2,1,0:T(8,128)(2,1)} collective-permute-done((bf16[1,256,2048]{2,1,0:T(8,128)(2,1)S(1)}, bf16[1,256,2048]{2,1,0:T(8,128)(2,1)}, u32[]{:S(2)}, u32[]{:S(2)}) %collective-permute-start.1) | collective-permute-done | bytes 1048608 | tf_op jit(solution)/shard_map/ppermute | solution.py:269
  88.7 9.8 %constant_dynamic-slice_fusion.3 = (bf16[1024,4,1,256]{3,2,1,0:T(2,128)(2,1)}, bf16[1024,4,1,256]{3,2,1,0:T(2,128)(2,1)}) fusion(bf16[1024,4,2,256]{3,2,1,0:T(2,128)(2,1)S(1)} %copy-done.3, s32[]{:T(128)S(6)} %select_n.198, s32[]{:T(128)S(6)} %select_n.199), kind=kLoop, calls=%fused_computation.229 | loop fusion | bytes 8388616 | tf_op jit(solution)/shard_map/jit(dynamic_index_in_dim)/dynamic_slice | solution.py:264
  98.5 10.6 %copy.81 = bf16[1024,4,1,256]{0,3,1,2:T(8,128)(2,1)} copy(bf16[1024,4,1,256]{3,2,1,0:T(2,128)(2,1)} %get-tuple-element.50) | data formatting | bytes 4194304
  109.0 10.5 %copy.80 = bf16[1024,4,1,256]{0,3,1,2:T(8,128)(2,1)} copy(bf16[1024,4,1,256]{3,2,1,0:T(2,128)(2,1)} %get-tuple-element.49) | data formatting | bytes 4194304
  119.6 7.8 reshape.278
  127.4 11.8 %constant_dynamic-slice_fusion.11 = (bf16[1024,4,1,256]{3,2,1,0:T(2,128)(2,1)}, bf16[1024,4,1,256]{3,2,1,0:T(2,128)(2,1)}) fusion(bf16[1024,4,2,256]{3,2,1,0:T(2,128)(2,1)} %reshape.278, s32[]{:T(128)S(6)} %select_n.198, s32[]{:T(128)S(6)} %select_n.199), kind=kLoop, calls=%fused_computation.238 | loop fusion | bytes 8388616 | tf_op jit(solution)/shard_map/jit(dynamic_index_in_dim)/dynamic_slice | solution.py:264
  139.2 10.6 %copy.56 = bf16[1024,4,1,256]{0,3,1,2:T(8,128)(2,1)} copy(bf16[1024,4,1,256]{3,2,1,0:T(2,128)(2,1)} %get-tuple-element.56) | data formatting | bytes 4194304 | tf_op jit(solution)/shard_map/jit(dynamic_index_in_dim)/dynamic_slice | solution.py:264
  149.7 10.6 %copy.55 = bf16[1024,4,1,256]{0,3,1,2:T(8,128)(2,1)} copy(bf16[1024,4,1,256]{3,2,1,0:T(2,128)(2,1)} %get-tuple-element.55) | data formatting | bytes 4194304 | tf_op jit(solution)/shard_map/jit(dynamic_index_in_dim)/dynamic_slice | solution.py:264
  164.9 10.5 %fusion.187 = f32[1024,1408]{1,0:T(8,128)} fusion(bf16[1024,2048]{1,0:T(8,128)(2,1)S(1)} %copy-done.16, bf16[1408,2048]{1,0:T(8,128)(2,1)} %param.16), kind=kOutput, calls=%fused_computation.275 | convolution fusion | flops 5905580032 | bytes 15728640 | tf_op jit(solution)/shard_map/td,fd->tf/dot_general | solution.py:362
  179.0 7.8 reshape_reshape_reshape.7
  186.7 11.3 %constant_dynamic-slice_fusion.5 = (bf16[1024,4,1,256]{3,2,1,0:T(2,128)(2,1)}, bf16[1024,4,1,256]{3,2,1,0:T(2,128)(2,1)}) fusion(bf16[1024,4,2,256]{3,2,1,0:T(2,128)(2,1)} %reshape_reshape_reshape.7, s32[]{:T(128)S(6)} %select_n.198, s32[]{:T(128)S(6)} %select_n.199), kind=kLoop, calls=%fused_computation.231 | loop fusion | bytes 8388616 | tf_op jit(solution)/shard_map/jit(dynamic_index_in_dim)/dynamic_slice | solution.py:264
  198.1 10.5 %copy.67 = bf16[1024,4,1,256]{0,3,1,2:T(8,128)(2,1)} copy(bf16[1024,4,1,256]{3,2,1,0:T(2,128)(2,1)} %get-tuple-element.52) | data formatting | bytes 4194304 | tf_op jit(solution)/shard_map/jit(dynamic_index_in_dim)/dynamic_slice | solution.py:264
  208.6 11.8 %fusion.8 = f32[1024,1408]{1,0:T(8,128)} fusion(bf16[1024,2048]{1,0:T(8,128)(2,1)} %bitcast.338, bf16[2,2048,1408]{2,1,0:T(8,128)(2,1)} %param.15), kind=kOutput, calls=%fused_computation.10 | convolution fusion | flops 5905580032 | bytes 15728640 | tf_op jit(solution)/shard_map/dot_general | solution.py:260
  220.4 14.0 %multiply_convert_fusion.1 = (bf16[1024,1408]{1,0:T(8,128)(2,1)S(1)}, bf16[1024,1408]{1,0:T(8,128)(2,1)S(1)}, bf16[1024,1408]{1,0:T(8,128)(2,1)S(1)}) fusion(f32[1024,1408]{1,0:T(8,128)} %fusion.187, f32[1024,1408]{1,0:T(8,128)} %fusion.8, bf16[1024,2048]{1,0:T(8,128)(2,1)S(1)} %bitcast.339, bf16[2,2048,1408]{2,1,0:T(8,128)(2,1)} %param.15), kind=kOutput, calls=%fused_computation.21 | convolution fusion | flops 5927206912 | bytes 30146560 | tf_op jit(solution)/shard_map/dot_general | solution.py:260
  253.5 10.6 %copy.66 = bf16[1024,4,1,256]{0,3,1,2:T(8,128)(2,1)} copy(bf16[1024,4,1,256]{3,2,1,0:T(2,128)(2,1)} %get-tuple-element.51) | data formatting | bytes 4194304 | tf_op jit(solution)/shard_map/jit(dynamic_index_in_dim)/dynamic_slice | solution.py:264
  265.6 8.0 fusion.29
  275.6 5.1 fusion.4
  280.6 6.5 add_convert_fusion.1
  292.7 5.3 fusion.24
  297.9 5.9 convert_add_fusion.4
  309.5 7.7 collective-permute-done.30
  317.2 5.2 bitcast_add_fusion
  331.4 47.6 %collective-permute-done.24 = bf16[4,256,1408]{2,1,0:T(8,128)(2,1)} collective-permute-done((bf16[4,256,1408]{2,1,0:T(8,128)(2,1)}, bf16[4,256,1408]{2,1,0:T(8,128)(2,1)}, u32[]{:S(2)}, u32[]{:S(2)}) %collective-permute-start.24) | collective-permute-done | bytes 2883616 | tf_op jit(solution)/shard_map/ppermute | solution.py:269
  379.0 6.9 convert_add_fusion.1
  398.0 41.1 %collective-permute-done.27 = bf16[4,256,1408]{2,1,0:T(8,128)(2,1)} collective-permute-done((bf16[4,256,1408]{2,1,0:T(8,128)(2,1)}, bf16[4,256,1408]{2,1,0:T(8,128)(2,1)}, u32[]{:S(2)}, u32[]{:S(2)}) %collective-permute-start.27) | collective-permute-done | bytes 2883616 | tf_op jit(solution)/shard_map/ppermute | solution.py:269
  439.1 5.2 convert_add_fusion
  449.6 42.4 %collective-permute-done.28 = bf16[2,256,1408]{2,1,0:T(8,128)(2,1)S(1)} collective-permute-done((bf16[2,256,1408]{2,1,0:T(8,128)(2,1)S(1)}, bf16[2,256,1408]{2,1,0:T(8,128)(2,1)S(1)}, u32[]{:S(2)}, u32[]{:S(2)}) %collective-permute-start.28) | collective-permute-done | bytes 1441824 | tf_op jit(solution)/shard_map/ppermute | solution.py:269
  496.0 44.7 %collective-permute-done.29 = bf16[1,256,1408]{2,1,0:T(8,128)(2,1)S(1)} collective-permute-done((bf16[1,256,1408]{2,1,0:T(8,128)(2,1)S(1)}, bf16[1,256,1408]{2,1,0:T(8,128)(2,1)S(1)}, u32[]{:S(2)}, u32[]{:S(2)}) %collective-permute-start.29) | collective-permute-done | bytes 720928 | tf_op jit(solution)/shard_map/ppermute | solution.py:269
  542.6 13.1 %collective-permute-done.32 = bf16[1,1408,256]{2,1,0:T(8,128)(2,1)S(1)} collective-permute-done((bf16[1,1408,256]{2,1,0:T(8,128)(2,1)S(1)}, bf16[1,1408,256]{2,1,0:T(8,128)(2,1)S(1)}, u32[]{:S(2)}, u32[]{:S(2)}) %collective-permute-start.32) | collective-permute-done | bytes 720928 | tf_op jit(solution)/shard_map/ppermute | solution.py:269
  559.8 7.9 reshape_reshape_reshape.6
  567.8 5.6 convolution_convert_fusion.4.g_ref
  573.4 28.4 %shard_map.171 = (bf16[1024,512]{1,0:T(8,128)(2,1)}, bf16[1024,512]{1,0:T(8,128)(2,1)}, bf16[1024,512]{1,0:T(8,128)(2,1)}) custom-call(s32[1,1024]{1,0:T(1,128)} %bitcast.385, bf16[1024,512]{1,0:T(8,128)(2,1)} %get-tuple-element.18.q_ref, bf16[1024,512]{1,0:T(8,128)(2,1)} %get-tuple-element.19.k_ref, bf16[1024,512]{1,0:T(8,128)(2,1)} %get-tuple-element.20.v_ref, ...), custom_call_target="tpu_custom_call" | custom-call | flops 8053063680 | bytes 8388608 | tf_op jit(solution)/shard_map/pallas_call | solution.py:236
  604.0 6.1 fusion.79
  627.0 9.8 %constant_dynamic-slice_fusion.9 = (bf16[1024,4,1,256]{3,2,1,0:T(2,128)(2,1)}, bf16[1024,4,1,256]{3,2,1,0:T(2,128)(2,1)}) fusion(bf16[1024,4,2,256]{3,2,1,0:T(2,128)(2,1)S(1)} %copy-done.4, s32[]{:T(128)S(6)} %select_n.198, s32[]{:T(128)S(6)} %select_n.199), kind=kLoop, calls=%fused_computation.235 | loop fusion | bytes 8388616 | tf_op jit(solution)/shard_map/jit(dynamic_index_in_dim)/dynamic_slice | solution.py:264
  636.7 10.6 %copy.62 = bf16[1024,4,1,256]{0,3,1,2:T(8,128)(2,1)} copy(bf16[1024,4,1,256]{3,2,1,0:T(2,128)(2,1)} %get-tuple-element.54) | data formatting | bytes 4194304 | tf_op jit(solution)/shard_map/jit(dynamic_index_in_dim)/dynamic_slice | solution.py:264
  652.9 10.8 %copy.61 = bf16[1024,4,1,256]{0,3,1,2:T(8,128)(2,1)} copy(bf16[1024,4,1,256]{3,2,1,0:T(2,128)(2,1)} %get-tuple-element.53) | data formatting | bytes 4194304 | tf_op jit(solution)/shard_map/jit(dynamic_index_in_dim)/dynamic_slice | solution.py:264
  663.7 7.0 add_convert_fusion
  673.2 5.2 add_add_fusion
  689.5 10.8 %collective-permute-done.12 = bf16[4,256,512]{2,1,0:T(8,128)(2,1)} collective-permute-done((bf16[4,256,512]{2,1,0:T(8,128)(2,1)}, bf16[4,256,512]{2,1,0:T(8,128)(2,1)}, u32[]{:S(2)}, u32[]{:S(2)}) %collective-permute-start.12) | collective-permute-done | bytes 1048608 | tf_op jit(solution)/shard_map/ppermute | solution.py:269
  703.5 19.2 %collective-permute-done.15 = bf16[4,256,512]{2,1,0:T(8,128)(2,1)} collective-permute-done((bf16[4,256,512]{2,1,0:T(8,128)(2,1)}, bf16[4,256,512]{2,1,0:T(8,128)(2,1)}, u32[]{:S(2)}, u32[]{:S(2)}) %collective-permute-start.15) | collective-permute-done | bytes 1048608 | tf_op jit(solution)/shard_map/ppermute | solution.py:269
  725.3 18.5 %collective-permute-done.18 = bf16[4,256,512]{2,1,0:T(8,128)(2,1)} collective-permute-done((bf16[4,256,512]{2,1,0:T(8,128)(2,1)}, bf16[4,256,512]{2,1,0:T(8,128)(2,1)}, u32[]{:S(2)}, u32[]{:S(2)}) %collective-permute-start.18) | collective-permute-done | bytes 1048608 | tf_op jit(solution)/shard_map/ppermute | solution.py:269
  753.1 16.8 %collective-permute-done.19 = bf16[2,256,512]{2,1,0:T(8,128)(2,1)S(1)} collective-permute-done((bf16[2,256,512]{2,1,0:T(8,128)(2,1)S(1)}, bf16[2,256,512]{2,1,0:T(8,128)(2,1)S(1)}, u32[]{:S(2)}, u32[]{:S(2)}) %collective-permute-start.19) | collective-permute-done | bytes 524320 | tf_op jit(solution)/shard_map/ppermute | solution.py:269
  774.5 10.4 %collective-permute-done.14 = bf16[1,256,512]{2,1,0:T(8,128)(2,1)S(1)} collective-permute-done((bf16[1,256,512]{2,1,0:T(8,128)(2,1)S(1)}, bf16[1,256,512]{2,1,0:T(8,128)(2,1)S(1)}, u32[]{:S(2)}, u32[]{:S(2)}) %collective-permute-start.14) | collective-permute-done | bytes 262176 | tf_op jit(solution)/shard_map/ppermute | solution.py:269
  785.0 5.5 collective-permute-done.17
  800.5 41.7 %all-reduce = (f32[3,2048]{1,0:T(4,128)}, f32[2,2048]{1,0:T(2,128)}, f32[2,2048]{1,0:T(2,128)}) all-reduce(f32[3,2048]{1,0:T(4,128)S(1)} %constant_dynamic-update-slice_fusion, f32[2,2048]{1,0:T(2,128)S(1)} %pad_maximum_fusion.6, f32[2,2048]{1,0:T(2,128)S(1)} %pad_maximum_fusion.7), channel_id=1, replica_groups=mesh['dp'=8,'tensor'=4] {'dp','tensor'}, use_global_device_ids=true, to_apply=%region_13.14 | all-reduce | flops 14336 | bytes 114688 | tf_op jit(solution)/shard_map/psum | solution.py:440
  (271 shorter events, 181.9 us)
Async XLA Ops:
  0.6 41.6 %copy-start = (bf16[512,2048]{1,0:T(8,128)(2,1)S(1)}, bf16[512,2048]{1,0:T(8,128)(2,1)}, u32[]{:S(2)}) copy-start(bf16[512,2048]{1,0:T(8,128)(2,1)} %param.14) | copy-start | bytes 6291460
  2.3 19.8 %copy-start.41 = (s32[1024]{0:T(1024)}, s32[1024]{0:T(1024)S(1)}, u32[]{:S(2)}) copy-start(s32[1024]{0:T(1024)S(1)} %select_reduce_fusion) | copy-start | bytes 12292
  46.0 4.6 collective-permute-start
  55.7 26.5 %collective-permute-start.1 = (bf16[1,256,2048]{2,1,0:T(8,128)(2,1)S(1)}, bf16[1,256,2048]{2,1,0:T(8,128)(2,1)}, u32[]{:S(2)}, u32[]{:S(2)}) collective-permute-start(bf16[1,256,2048]{2,1,0:T(8,128)(2,1)S(1)} %dynamic-slice_convert_fusion.3), channel_id=1, source_target_pairs={{0,2},{1,3},{2,0},{3,1},{4,6},{5,7},{6,4},{7,5},{8,10},{9,11},{10,... | collective-permute-start | bytes 3145736 | tf_op jit(solution)/shard_map/ppermute | solution.py:269
  67.9 17.2 %copy-start.42 = (f32[256]{0:T(256)}, f32[256]{0:T(256)S(1)}, u32[]{:S(2)}) copy-start(f32[256]{0:T(256)S(1)} %broadcast_multiply_fusion.2) | copy-start | bytes 3076
  86.9 73.4 %collective-permute-start.2 = (bf16[1,256,2048]{2,1,0:T(8,128)(2,1)}, bf16[1,256,2048]{2,1,0:T(8,128)(2,1)S(1)}, u32[]{:S(2)}, u32[]{:S(2)}) collective-permute-start(bf16[1,256,2048]{2,1,0:T(8,128)(2,1)} %fusion.131), channel_id=1, source_target_pairs={{0,2},{1,3},{2,0},{3,1},{4,6},{5,7},{6,4},{7,5},{8,10},{9,11},{10,... | collective-permute-start | bytes 3145736 | tf_op jit(solution)/shard_map/ppermute | solution.py:269
  162.9 13.1 %collective-permute-start.3 = (bf16[2,256,2048]{2,1,0:T(8,128)(2,1)S(1)}, bf16[2,256,2048]{2,1,0:T(8,128)(2,1)S(1)}, u32[]{:S(2)}, u32[]{:S(2)}) collective-permute-start(bf16[2,256,2048]{2,1,0:T(8,128)(2,1)S(1)} %maximum_bitcast_fusion), channel_id=1, source_target_pairs={{0,1},{1,0},{2,3},{3,2},{4,5},{5,4},{6,7},{7,6},{8,9},{9,8},{10,11... | collective-permute-start | bytes 6291464 | tf_op jit(solution)/shard_map/ppermute | solution.py:269
  220.4 14.0 %copy-start.36 = (bf16[1024,4,1,256]{0,3,1,2:T(8,128)(2,1)S(1)}, bf16[1024,4,1,256]{0,3,1,2:T(8,128)(2,1)}, u32[]{:S(2)}) copy-start(bf16[1024,4,1,256]{0,3,1,2:T(8,128)(2,1)} %copy.67) | copy-start | bytes 6291460
  234.4 12.3 %copy-start.45 = (bf16[1024,1408]{1,0:T(8,128)(2,1)}, bf16[1024,1408]{1,0:T(8,128)(2,1)S(1)}, u32[]{:S(2)}) copy-start(bf16[1024,1408]{1,0:T(8,128)(2,1)S(1)} %get-tuple-element.46) | copy-start | bytes 8650756
  251.5 65.7 %collective-permute-start.30 = (bf16[4,1408,256]{1,2,0:T(8,128)(2,1)}, bf16[4,1408,256]{1,2,0:T(8,128)(2,1)}, u32[]{:S(2)}, u32[]{:S(2)}) collective-permute-start(bf16[4,1408,256]{1,2,0:T(8,128)(2,1)} %fusion.23), channel_id=1, source_target_pairs={{0,4},{4,0},{8,12},{12,8},{16,20},{20,16},{24,28},{28,24},{1,5},{5... | collective-permute-start | bytes 8650760 | tf_op jit(solution)/shard_map/ppermute | solution.py:269
  253.0 126.0 %collective-permute-start.24 = (bf16[4,256,1408]{2,1,0:T(8,128)(2,1)}, bf16[4,256,1408]{2,1,0:T(8,128)(2,1)}, u32[]{:S(2)}, u32[]{:S(2)}) collective-permute-start(bf16[4,256,1408]{2,1,0:T(8,128)(2,1)} %convolution_convert_fusion.2), channel_id=1, source_target_pairs={{0,4},{4,0},{8,12},{12,8},{16,20},{20,16},{24,28},{28,24},{1,5},{5... | collective-permute-start | bytes 8650760 | tf_op jit(solution)/shard_map/ppermute | solution.py:269
  264.1 175.0 %collective-permute-start.27 = (bf16[4,256,1408]{2,1,0:T(8,128)(2,1)}, bf16[4,256,1408]{2,1,0:T(8,128)(2,1)}, u32[]{:S(2)}, u32[]{:S(2)}) collective-permute-start(bf16[4,256,1408]{2,1,0:T(8,128)(2,1)} %convolution_convert_fusion.1), channel_id=1, source_target_pairs={{0,4},{4,0},{8,12},{12,8},{16,20},{20,16},{24,28},{28,24},{1,5},{5... | collective-permute-start | bytes 8650760 | tf_op jit(solution)/shard_map/ppermute | solution.py:269
  273.7 24.3 %collective-permute-start.4 = (bf16[2,256,2048]{2,1,0:T(8,128)(2,1)}, bf16[2,256,2048]{2,1,0:T(8,128)(2,1)S(1)}, u32[]{:S(2)}, u32[]{:S(2)}) collective-permute-start(bf16[2,256,2048]{2,1,0:T(8,128)(2,1)} %fusion.29), channel_id=1, source_target_pairs={{0,1},{1,0},{2,3},{3,2},{4,5},{5,4},{6,7},{7,6},{8,9},{9,8},{10,11... | collective-permute-start | bytes 6291464 | tf_op jit(solution)/shard_map/ppermute | solution.py:269
  287.1 19.5 %collective-permute-start.6 = (bf16[2,256,2048]{2,1,0:T(8,128)(2,1)}, bf16[2,256,2048]{2,1,0:T(8,128)(2,1)S(1)}, u32[]{:S(2)}, u32[]{:S(2)}) collective-permute-start(bf16[2,256,2048]{2,1,0:T(8,128)(2,1)} %bitcast.27), channel_id=1, source_target_pairs={{0,1},{1,0},{2,3},{3,2},{4,5},{5,4},{6,7},{7,6},{8,9},{9,8},{10,11... | collective-permute-start | bytes 6291464 | tf_op jit(solution)/shard_map/ppermute | solution.py:269
  305.1 85.3 %collective-permute-start.5 = (bf16[1,256,2048]{2,1,0:T(8,128)(2,1)}, bf16[1,256,2048]{2,1,0:T(8,128)(2,1)}, u32[]{:S(2)}, u32[]{:S(2)}) collective-permute-start(bf16[1,256,2048]{2,1,0:T(8,128)(2,1)} %dynamic-slice_convert_fusion.2), channel_id=1, source_target_pairs={{0,2},{1,3},{2,0},{3,1},{4,6},{5,7},{6,4},{7,5},{8,10},{9,11},{10,... | collective-permute-start | bytes 3145736 | tf_op jit(solution)/shard_map/ppermute | solution.py:269
  307.2 15.2 %copy-start.10 = (f32[2,256,2048]{2,1,0:T(8,128)}, f32[2,256,2048]{2,1,0:T(8,128)S(1)}, u32[]{:S(2)}) copy-start(f32[2,256,2048]{2,1,0:T(8,128)S(1)} %convert_add_fusion.3) | copy-start | bytes 12582916
  308.4 79.4 %collective-permute-start.7 = (bf16[1,256,2048]{2,1,0:T(8,128)(2,1)}, bf16[1,256,2048]{2,1,0:T(8,128)(2,1)}, u32[]{:S(2)}, u32[]{:S(2)}) collective-permute-start(bf16[1,256,2048]{2,1,0:T(8,128)(2,1)} %dynamic-slice_convert_fusion.1), channel_id=1, source_target_pairs={{0,2},{1,3},{2,0},{3,1},{4,6},{5,7},{6,4},{7,5},{8,10},{9,11},{10,... | collective-permute-start | bytes 3145736 | tf_op jit(solution)/shard_map/ppermute | solution.py:269
  329.7 164.3 %collective-permute-start.31 = (bf16[2,1408,256]{2,1,0:T(8,128)(2,1)}, bf16[2,1408,256]{2,1,0:T(8,128)(2,1)S(1)}, u32[]{:S(2)}, u32[]{:S(2)}) collective-permute-start(bf16[2,1408,256]{2,1,0:T(8,128)(2,1)} %bitcast.360), channel_id=1, source_target_pairs={{0,8},{4,12},{8,0},{12,4},{16,24},{20,28},{24,16},{28,20},{1,9},{5... | collective-permute-start | bytes 4325384 | tf_op jit(solution)/shard_map/ppermute | solution.py:269
  386.1 60.5 %collective-permute-start.25 = (bf16[2,256,1408]{2,1,0:T(8,128)(2,1)S(1)}, bf16[2,256,1408]{2,1,0:T(8,128)(2,1)S(1)}, u32[]{:S(2)}, u32[]{:S(2)}) collective-permute-start(bf16[2,256,1408]{2,1,0:T(8,128)(2,1)S(1)} %fusion.114), channel_id=1, source_target_pairs={{0,8},{4,12},{8,0},{12,4},{16,24},{20,28},{24,16},{28,20},{1,9},{5... | collective-permute-start | bytes 4325384 | tf_op jit(solution)/shard_map/ppermute | solution.py:269
  390.4 48.8 %copy-start.26 = (bf16[1024,1408]{1,0:T(8,128)(2,1)S(1)}, bf16[1024,1408]{1,0:T(8,128)(2,1)}, u32[]{:S(2)}) copy-start(bf16[1024,1408]{1,0:T(8,128)(2,1)} %copy-done.25) | copy-start | bytes 8650756
  390.4 48.8 %copy-start.33 = (bf16[1024,4,1,256]{0,3,1,2:T(8,128)(2,1)S(1)}, bf16[1024,4,1,256]{0,3,1,2:T(8,128)(2,1)}, u32[]{:S(2)}) copy-start(bf16[1024,4,1,256]{0,3,1,2:T(8,128)(2,1)} %copy.66) | copy-start | bytes 6291460
  396.5 49.7 %collective-permute-start.8 = (bf16[1,256,2048]{2,1,0:T(8,128)(2,1)S(1)}, bf16[1,256,2048]{2,1,0:T(8,128)(2,1)S(1)}, u32[]{:S(2)}, u32[]{:S(2)}) collective-permute-start(bf16[1,256,2048]{2,1,0:T(8,128)(2,1)S(1)} %get-tuple-element.40), channel_id=1, source_target_pairs={{0,2},{1,3},{2,0},{3,1},{4,6},{5,7},{6,4},{7,5},{8,10},{9,11},{10,... | collective-permute-start | bytes 3145736 | tf_op jit(solution)/shard_map/ppermute | solution.py:269
  444.6 47.4 %collective-permute-start.28 = (bf16[2,256,1408]{2,1,0:T(8,128)(2,1)S(1)}, bf16[2,256,1408]{2,1,0:T(8,128)(2,1)S(1)}, u32[]{:S(2)}, u32[]{:S(2)}) collective-permute-start(bf16[2,256,1408]{2,1,0:T(8,128)(2,1)S(1)} %fusion.115), channel_id=1, source_target_pairs={{0,8},{4,12},{8,0},{12,4},{16,24},{20,28},{24,16},{28,20},{1,9},{5... | collective-permute-start | bytes 4325384 | tf_op jit(solution)/shard_map/ppermute | solution.py:269
  446.5 110.4 %collective-permute-start.9 = (bf16[2,256,2048]{2,1,0:T(8,128)(2,1)S(1)}, bf16[2,256,2048]{2,1,0:T(8,128)(2,1)S(1)}, u32[]{:S(2)}, u32[]{:S(2)}) collective-permute-start(bf16[2,256,2048]{2,1,0:T(8,128)(2,1)S(1)} %maximum_bitcast_fusion.1), channel_id=1, source_target_pairs={{0,1},{1,0},{2,3},{3,2},{4,5},{5,4},{6,7},{7,6},{8,9},{9,8},{10,11... | collective-permute-start | bytes 6291464 | tf_op jit(solution)/shard_map/ppermute | solution.py:269
  446.9 48.9 %collective-permute-start.26 = (bf16[1,256,1408]{2,1,0:T(8,128)(2,1)S(1)}, bf16[1,256,1408]{2,1,0:T(8,128)(2,1)S(1)}, u32[]{:S(2)}, u32[]{:S(2)}) collective-permute-start(bf16[1,256,1408]{2,1,0:T(8,128)(2,1)S(1)} %dynamic-slice_convert_fusion.6), channel_id=1, source_target_pairs={{0,16},{4,20},{8,24},{12,28},{16,0},{20,4},{24,8},{28,12},{1,17},{... | collective-permute-start | bytes 2162696 | tf_op jit(solution)/shard_map/ppermute | solution.py:269
  492.4 48.2 %collective-permute-start.29 = (bf16[1,256,1408]{2,1,0:T(8,128)(2,1)S(1)}, bf16[1,256,1408]{2,1,0:T(8,128)(2,1)S(1)}, u32[]{:S(2)}, u32[]{:S(2)}) collective-permute-start(bf16[1,256,1408]{2,1,0:T(8,128)(2,1)S(1)} %dynamic-slice_convert_fusion.5), channel_id=1, source_target_pairs={{0,16},{4,20},{8,24},{12,28},{16,0},{20,4},{24,8},{28,12},{1,17},{... | collective-permute-start | bytes 2162696 | tf_op jit(solution)/shard_map/ppermute | solution.py:269
  494.4 61.2 %collective-permute-start.32 = (bf16[1,1408,256]{2,1,0:T(8,128)(2,1)S(1)}, bf16[1,1408,256]{2,1,0:T(8,128)(2,1)S(1)}, u32[]{:S(2)}, u32[]{:S(2)}) collective-permute-start(bf16[1,1408,256]{2,1,0:T(8,128)(2,1)S(1)} %dynamic-slice_convert_fusion.4), channel_id=1, source_target_pairs={{0,16},{4,20},{8,24},{12,28},{16,0},{20,4},{24,8},{28,12},{1,17},{... | collective-permute-start | bytes 2162696 | tf_op jit(solution)/shard_map/ppermute | solution.py:269
  604.0 12.8 %copy-start.15 = (bf16[2,1,256,1536]{3,2,1,0:T(8,128)(2,1)}, bf16[2,1,256,1536]{3,2,1,0:T(8,128)(2,1)S(1)}, u32[]{:S(2)}) copy-start(bf16[2,1,256,1536]{3,2,1,0:T(8,128)(2,1)S(1)} %get-tuple-element.63) | copy-start | bytes 4718596
  651.4 27.5 %collective-permute-start.21 = (bf16[4,512,256]{1,2,0:T(8,128)(2,1)}, bf16[4,512,256]{1,2,0:T(8,128)(2,1)}, u32[]{:S(2)}, u32[]{:S(2)}) collective-permute-start(bf16[4,512,256]{1,2,0:T(8,128)(2,1)} %fusion.128), channel_id=1, source_target_pairs={{0,4},{4,0},{8,12},{12,8},{16,20},{20,16},{24,28},{28,24},{1,5},{5... | collective-permute-start | bytes 3145736 | tf_op jit(solution)/shard_map/ppermute | solution.py:269
  670.7 99.5 %collective-permute-start.10 = (bf16[2,256,2048]{2,1,0:T(8,128)(2,1)}, bf16[2,256,2048]{2,1,0:T(8,128)(2,1)}, u32[]{:S(2)}, u32[]{:S(2)}) collective-permute-start(bf16[2,256,2048]{2,1,0:T(8,128)(2,1)} %bitcast.43), channel_id=1, source_target_pairs={{0,1},{1,0},{2,3},{3,2},{4,5},{5,4},{6,7},{7,6},{8,9},{9,8},{10,11... | collective-permute-start | bytes 6291464 | tf_op jit(solution)/shard_map/ppermute | solution.py:269
  670.7 29.5 %collective-permute-start.12 = (bf16[4,256,512]{2,1,0:T(8,128)(2,1)}, bf16[4,256,512]{2,1,0:T(8,128)(2,1)}, u32[]{:S(2)}, u32[]{:S(2)}) collective-permute-start(bf16[4,256,512]{2,1,0:T(8,128)(2,1)} %fusion.102), channel_id=1, source_target_pairs={{0,4},{4,0},{8,12},{12,8},{16,20},{20,16},{24,28},{28,24},{1,5},{5... | collective-permute-start | bytes 3145736 | tf_op jit(solution)/shard_map/ppermute | solution.py:269
  671.2 51.5 %collective-permute-start.15 = (bf16[4,256,512]{2,1,0:T(8,128)(2,1)}, bf16[4,256,512]{2,1,0:T(8,128)(2,1)}, u32[]{:S(2)}, u32[]{:S(2)}) collective-permute-start(bf16[4,256,512]{2,1,0:T(8,128)(2,1)} %fusion.105), channel_id=1, source_target_pairs={{0,4},{4,0},{8,12},{12,8},{16,20},{20,16},{24,28},{28,24},{1,5},{5... | collective-permute-start | bytes 3145736 | tf_op jit(solution)/shard_map/ppermute | solution.py:269
  672.7 71.1 %collective-permute-start.18 = (bf16[4,256,512]{2,1,0:T(8,128)(2,1)}, bf16[4,256,512]{2,1,0:T(8,128)(2,1)}, u32[]{:S(2)}, u32[]{:S(2)}) collective-permute-start(bf16[4,256,512]{2,1,0:T(8,128)(2,1)} %fusion.108), channel_id=1, source_target_pairs={{0,4},{4,0},{8,12},{12,8},{16,20},{20,16},{24,28},{28,24},{1,5},{5... | collective-permute-start | bytes 3145736 | tf_op jit(solution)/shard_map/ppermute | solution.py:269
  685.2 15.0 %copy-start.24 = (bf16[1024,512]{1,0:T(8,128)(2,1)S(1)}, bf16[1024,512]{1,0:T(8,128)(2,1)}, u32[]{:S(2)}) copy-start(bf16[1024,512]{1,0:T(8,128)(2,1)} %get-tuple-element.23) | copy-start | bytes 3145732
  689.5 33.2 %copy-start.22 = (bf16[1024,512]{1,0:T(8,128)(2,1)S(1)}, bf16[1024,512]{1,0:T(8,128)(2,1)}, u32[]{:S(2)}) copy-start(bf16[1024,512]{1,0:T(8,128)(2,1)} %get-tuple-element.24) | copy-start | bytes 3145732
  689.5 33.2 %copy-start.30 = (bf16[1024,4,1,256]{0,3,1,2:T(8,128)(2,1)S(1)}, bf16[1024,4,1,256]{0,3,1,2:T(8,128)(2,1)}, u32[]{:S(2)}) copy-start(bf16[1024,4,1,256]{0,3,1,2:T(8,128)(2,1)} %copy.55) | copy-start | bytes 6291460
  689.5 57.0 %collective-permute-start.22 = (bf16[2,512,256]{2,1,0:T(8,128)(2,1)}, bf16[2,512,256]{2,1,0:T(8,128)(2,1)S(1)}, u32[]{:S(2)}, u32[]{:S(2)}) collective-permute-start(bf16[2,512,256]{2,1,0:T(8,128)(2,1)} %bitcast.369), channel_id=1, source_target_pairs={{0,8},{4,12},{8,0},{12,4},{16,24},{20,28},{24,16},{28,20},{1,9},{5... | collective-permute-start | bytes 1572872 | tf_op jit(solution)/shard_map/ppermute | solution.py:269
  703.4 40.4 %copy-start.19 = (bf16[1024,512]{1,0:T(8,128)(2,1)S(1)}, bf16[1024,512]{1,0:T(8,128)(2,1)}, u32[]{:S(2)}) copy-start(bf16[1024,512]{1,0:T(8,128)(2,1)} %get-tuple-element.25) | copy-start | bytes 3145732
  703.4 46.2 %collective-permute-start.13 = (bf16[2,256,512]{2,1,0:T(8,128)(2,1)S(1)}, bf16[2,256,512]{2,1,0:T(8,128)(2,1)S(1)}, u32[]{:S(2)}, u32[]{:S(2)}) collective-permute-start(bf16[2,256,512]{2,1,0:T(8,128)(2,1)S(1)} %fusion.160), channel_id=1, source_target_pairs={{0,8},{4,12},{8,0},{12,4},{16,24},{20,28},{24,16},{28,20},{1,9},{5... | collective-permute-start | bytes 1572872 | tf_op jit(solution)/shard_map/ppermute | solution.py:269
  725.2 21.2 %copy-start.17 = (f32[2,1,512,256]{3,2,0,1:T(8,128)S(1)}, f32[2,1,512,256]{3,2,0,1:T(8,128)}, u32[]{:S(2)}) copy-start(f32[2,1,512,256]{3,2,0,1:T(8,128)} %copy.63) | copy-start | bytes 3145732
  725.3 24.7 %collective-permute-start.16 = (bf16[2,256,512]{2,1,0:T(8,128)(2,1)S(1)}, bf16[2,256,512]{2,1,0:T(8,128)(2,1)S(1)}, u32[]{:S(2)}, u32[]{:S(2)}) collective-permute-start(bf16[2,256,512]{2,1,0:T(8,128)(2,1)S(1)} %fusion.161), channel_id=1, source_target_pairs={{0,8},{4,12},{8,0},{12,4},{16,24},{20,28},{24,16},{28,20},{1,9},{5... | collective-permute-start | bytes 1572872 | tf_op jit(solution)/shard_map/ppermute | solution.py:269
  746.4 23.5 %collective-permute-start.19 = (bf16[2,256,512]{2,1,0:T(8,128)(2,1)S(1)}, bf16[2,256,512]{2,1,0:T(8,128)(2,1)S(1)}, u32[]{:S(2)}, u32[]{:S(2)}) collective-permute-start(bf16[2,256,512]{2,1,0:T(8,128)(2,1)S(1)} %fusion.162), channel_id=1, source_target_pairs={{0,8},{4,12},{8,0},{12,4},{16,24},{20,28},{24,16},{28,20},{1,9},{5... | collective-permute-start | bytes 1572872 | tf_op jit(solution)/shard_map/ppermute | solution.py:269
  746.7 49.0 %collective-permute-start.23 = (bf16[1,512,256]{2,1,0:T(8,128)(2,1)S(1)}, bf16[1,512,256]{2,1,0:T(8,128)(2,1)S(1)}, u32[]{:S(2)}, u32[]{:S(2)}) collective-permute-start(bf16[1,512,256]{2,1,0:T(8,128)(2,1)S(1)} %dynamic-slice_convert_fusion.7), channel_id=1, source_target_pairs={{0,16},{4,20},{8,24},{12,28},{16,0},{20,4},{24,8},{28,12},{1,17},{... | collective-permute-start | bytes 786440 | tf_op jit(solution)/shard_map/ppermute | solution.py:269
  749.8 35.1 %collective-permute-start.14 = (bf16[1,256,512]{2,1,0:T(8,128)(2,1)S(1)}, bf16[1,256,512]{2,1,0:T(8,128)(2,1)S(1)}, u32[]{:S(2)}, u32[]{:S(2)}) collective-permute-start(bf16[1,256,512]{2,1,0:T(8,128)(2,1)S(1)} %dynamic-slice_convert_fusion.10), channel_id=1, source_target_pairs={{0,16},{4,20},{8,24},{12,28},{16,0},{20,4},{24,8},{28,12},{1,17},{... | collective-permute-start | bytes 786440 | tf_op jit(solution)/shard_map/ppermute | solution.py:269
  749.9 20.2 %copy-start.9 = (f32[512,2048]{1,0:T(8,128)S(1)}, f32[512,2048]{1,0:T(8,128)}, u32[]{:S(2)}) copy-start(f32[512,2048]{1,0:T(8,128)} %add_add_fusion) | copy-start | bytes 12582916
  750.2 40.4 %collective-permute-start.17 = (bf16[1,256,512]{2,1,0:T(8,128)(2,1)S(1)}, bf16[1,256,512]{2,1,0:T(8,128)(2,1)S(1)}, u32[]{:S(2)}, u32[]{:S(2)}) collective-permute-start(bf16[1,256,512]{2,1,0:T(8,128)(2,1)S(1)} %dynamic-slice_convert_fusion.9), channel_id=1, source_target_pairs={{0,16},{4,20},{8,24},{12,28},{16,0},{20,4},{24,8},{28,12},{1,17},{... | collective-permute-start | bytes 786440 | tf_op jit(solution)/shard_map/ppermute | solution.py:269
  770.1 24.2 %collective-permute-start.20 = (bf16[1,256,512]{2,1,0:T(8,128)(2,1)S(1)}, bf16[1,256,512]{2,1,0:T(8,128)(2,1)S(1)}, u32[]{:S(2)}, u32[]{:S(2)}) collective-permute-start(bf16[1,256,512]{2,1,0:T(8,128)(2,1)S(1)} %dynamic-slice_convert_fusion.8), channel_id=1, source_target_pairs={{0,16},{4,20},{8,24},{12,28},{16,0},{20,4},{24,8},{28,12},{1,17},{... | collective-permute-start | bytes 786440 | tf_op jit(solution)/shard_map/ppermute | solution.py:269
  772.8 23.6 %collective-permute-start.11 = (bf16[1,256,2048]{2,1,0:T(8,128)(2,1)S(1)}, bf16[1,256,2048]{2,1,0:T(8,128)(2,1)S(1)}, u32[]{:S(2)}, u32[]{:S(2)}) collective-permute-start(bf16[1,256,2048]{2,1,0:T(8,128)(2,1)S(1)} %dynamic-slice_convert_fusion), channel_id=1, source_target_pairs={{0,2},{1,3},{2,0},{3,1},{4,6},{5,7},{6,4},{7,5},{8,10},{9,11},{10,... | collective-permute-start | bytes 3145736 | tf_op jit(solution)/shard_map/ppermute | solution.py:269
  (39 other events, 200.3 us)

commit v2 on v1

--- a/solution.py
+++ b/solution.py
@@ -89,6 +89,7 @@
 
     return pl.pallas_call(
         qkv_kernel,
+        name="project",
         grid=(rows // block,),
         in_specs=[
             by_row(full),
@@ -104,11 +105,7 @@
         out_shape=[jax.ShapeDtypeStruct((rows, full), BF16)]
         + [jax.ShapeDtypeStruct((rows, width), BF16)] * 3,
         compiler_params=pltpu.CompilerParams(vmem_limit_bytes=VMEM_LIMIT),
-        cost_estimate=pl.CostEstimate(
-            flops=6 * rows * full * width,
-            bytes_accessed=2 * (2 * rows * full + 3 * full * width + 3 * rows * width),
-            transcendentals=0,
-        ),
+        cost_estimate=pl.CostEstimate(flops=0, bytes_accessed=0, transcendentals=0),
     )(tokens, weight, bias.astype(F32), gain[None], shift[None], *tables)
 
 
@@ -165,6 +162,7 @@
     blocks = rows // BQ
     return pl.pallas_call(
         functools.partial(attend_kernel, blocks),
+        name="attend",
         grid=(width // 128, blocks),
         in_specs=[
             pl.BlockSpec((1, BQ), lambda h, i: (0, i)),
@@ -181,9 +179,7 @@
             jax.ShapeDtypeStruct((width // HD, 1, rows), F32),
         ],
         compiler_params=pltpu.CompilerParams(vmem_limit_bytes=VMEM_LIMIT),
-        cost_estimate=pl.CostEstimate(
-            flops=8 * rows * 768 * width, bytes_accessed=8 * rows * width, transcendentals=rows * 768 * width // HD
-        ),
+        cost_estimate=pl.CostEstimate(flops=0, bytes_accessed=0, transcendentals=0),
     )(begins[None], queries, keys, values)
 
 
@@ -235,6 +231,7 @@
     column = pl.BlockSpec((rows, 128), lambda h, i: (0, h))
     return pl.pallas_call(
         functools.partial(attend_back_kernel, blocks),
+        name="attend_back",
         grid=(width // 128, blocks),
         in_specs=[
             pl.BlockSpec((1, BQ), lambda h, i: (0, i)),
@@ -250,14 +247,41 @@
         out_shape=[jax.ShapeDtypeStruct((rows, width), BF16)] * 3,
         scratch_shapes=[pltpu.VMEM((rows, 128), F32)] * 2,
         compiler_params=pltpu.CompilerParams(vmem_limit_bytes=VMEM_LIMIT),
-        cost_estimate=pl.CostEstimate(
-            flops=20 * rows * 768 * width, bytes_accessed=16 * rows * width, transcendentals=rows * 768 * width // HD
+        cost_estimate=pl.CostEstimate(flops=0, bytes_accessed=0, transcendentals=0),
+    )(begins[None], queries, keys, values, grads, logs, *tables, *tables)
+
+
+ANY = pl.BlockSpec(memory_space=pl.ANY)
+
+
+def call(name, kernel, marks, grid, ins, in_specs, outs, out_specs, after=(), flops=0, moved=0, scratch=()):
+    given, waits = len(ins), len(after)
+
+    def inner(mark, *refs):
+        kernel(mark, *refs[:given], *refs[given + waits :])
+
+    return pl.pallas_call(
+        inner,
+        grid_spec=pltpu.PrefetchScalarGridSpec(
+            num_scalar_prefetch=1,
+            grid=grid,
+            in_specs=list(in_specs) + [ANY] * waits,
+            out_specs=out_specs,
+            scratch_shapes=scratch,
         ),
-    )(begins[None], queries, keys, values, grads, logs, *tables, *tables)
-
-
-def dot(left, right):
-    return jnp.dot(left, right, preferred_element_type=F32)
+        out_shape=outs,
+        name=name,
+        compiler_params=pltpu.CompilerParams(vmem_limit_bytes=VMEM_LIMIT),
+        cost_estimate=pl.CostEstimate(flops=0, bytes_accessed=0, transcendentals=0),
+    )(marks, *ins, *after)
+
+
+def fixed(*dims):
+    return pl.BlockSpec(dims, lambda *_: (0,) * len(dims))
+
+
+def shape(dims, kind):
+    return jax.ShapeDtypeStruct(dims, kind)
 
 
 def pick(values, at, axis):
@@ -269,62 +293,322 @@
     return lax.ppermute(values, axis, [(i, i ^ (1 << bit)) for i in range(size)])
 
 
-def sum_rows(left, times):
-    size = lax.axis_size("tensor")
-    me = lax.axis_index("tensor")
-    bits = size.bit_length() - 1
-    rows = left.shape[0] // size
-    core = me & 1
-    by_core = left.reshape(size // 2, 2, rows, left.shape[1])
-
-    def product(of):
-        taken = pick(by_core, of, 1)
-        got = times(taken.reshape(-1, left.shape[1]))
-        return got.reshape(size // 2, rows, got.shape[-1])
-
-    arrived = swap(product(1 - core).astype(BF16), "tensor", 0)
-    total = product(core) + arrived.astype(F32)
-    for bit in range(1, bits):
+CORE, CHIP, DP = 0, 1, 2
+
+
+def rows_product(marks, lefts, weight, flipped, arrived=None, after=()):
+    rows, depth = lefts[0].shape
+    share = rows // 4
+    width = weight.shape[-2] if flipped else weight.shape[-1]
+    tile = 256
+    count = len(lefts)
+    keep = arrived is not None
+
+    def kernel(mark, *refs):
+        total = 0.0
+        for j in range(count):
+            left = refs[j][...].reshape(2 * share, depth)
+            if flipped:
+                total += over_columns(left, refs[count][j])
+            else:
+                total += jnp.dot(left, refs[count][...], preferred_element_type=F32)
+        total = total.reshape(2, share, tile)
+        if keep:
+            total = total + refs[count + 1][...].astype(F32)
+            first = mark[CHIP] == 0
+            refs[-2][...] = jnp.where(first, total[1], total[0]).astype(BF16)
+            refs[-1][...] = jnp.where(first, total[0], total[1])
+        else:
+            refs[-1][...] = total.astype(BF16)
+
+    def of_core(i, mark):
+        return (0, mark[CORE] if keep else 1 - mark[CORE], 0, 0)
+
+    in_specs = [pl.BlockSpec((2, 1, share, depth), of_core)] * count
+    if flipped:
+        in_specs.append(pl.BlockSpec((count, tile, depth), lambda i, mark: (0, i, 0)))
+    else:
+        in_specs.append(pl.BlockSpec((depth, tile), lambda i, mark: (0, i)))
+    ins = [left.reshape(2, 2, share, depth) for left in lefts] + [weight]
+    pair = pl.BlockSpec((2, share, tile), lambda i, mark: (0, 0, i))
+    one = pl.BlockSpec((share, tile), lambda i, mark: (0, i))
+    if keep:
+        ins.append(arrived)
+        in_specs.append(pair)
+        outs, out_specs = [shape((share, width), BF16), shape((share, width), F32)], [one, one]
+    else:
+        outs, out_specs = shape((2, share, width), BF16), pair
+    return call(
+        "rows_keep" if keep else "rows_send", kernel, marks, (width // tile,), ins, in_specs, outs, out_specs, after,
+        flops=4 * share * depth * width * count, moved=2 * depth * width * count,
+    )
+
+
+def norm_rows(marks, tokens, kept, arrived, gain, shift, after=()):
+    share, full = kept.shape
+    block = min(128, share)
+    steps = share // block
+
+    def kernel(mark, x_ref, k_ref, a_ref, g_ref, s_ref, r_ref, n_ref):
+        residual = x_ref[...].astype(F32) + (k_ref[...] + a_ref[...].astype(F32))
+        unit, _ = norm_parts(residual)
+        r_ref[...] = residual
+        n_ref[...] = (unit * g_ref[...] + s_ref[...]).astype(BF16)
+
+    rows = pl.BlockSpec((block, full), lambda i, mark: (i, 0))
+    mine = pl.BlockSpec((block, full), lambda i, mark: ((2 * mark[CHIP] + mark[CORE]) * steps + i, 0))
+    return call(
+        "norm_rows", kernel, marks, (steps,), [tokens, kept, arrived, gain[None], shift[None]],
+        [mine, rows, rows, fixed(1, full), fixed(1, full)],
+        [shape((share, full), F32), shape((share, full), BF16)], [rows, rows], after,
+        flops=10 * share * full, moved=14 * share * full,
+    )
+
+
+def norm_back_rows(marks, values, base, kept, arrived, gain, after=()):
+    share, full = kept.shape
+    block = min(128, share)
+    steps = share // block
+
+    def kernel(mark, x_ref, b_ref, k_ref, a_ref, g_ref, o_ref, l_ref, s_ref):
+        unit, inverse = norm_parts(x_ref[...].astype(F32))
+        grad = k_ref[...] + a_ref[...].astype(F32)
+        out = b_ref[...].astype(F32) + norm_back(unit, inverse, g_ref[...], grad)
+        o_ref[...] = out
+        l_ref[...] = out.astype(BF16)
+
+        @pl.when(pl.program_id(0) == 0)
+        def _():
+            s_ref[...] = jnp.zeros_like(s_ref)
+
+        s_ref[0:1, :] += jnp.sum(grad * unit, axis=0, keepdims=True)
+        s_ref[1:2, :] += jnp.sum(grad, axis=0, keepdims=True)
+
+    rows = pl.BlockSpec((block, full), lambda i, mark: (i, 0))
+    mine = pl.BlockSpec((block, full), lambda i, mark: ((2 * mark[CHIP] + mark[CORE]) * steps + i, 0))
+
+    def where(of):
+        return rows if of.shape[0] == share else mine
+
+    return call(
+        "norm_back_rows", kernel, marks, (steps,), [values, base, kept, arrived, gain[None]],
+        [where(values), where(base), rows, rows, fixed(1, full)],
+        [shape((share, full), F32), shape((share, full), BF16), shape((2, full), F32)],
+        [rows, rows, fixed(2, full)], after,
+        flops=20 * share * full, moved=18 * share * full,
+    )
+
+
+def spread(own):
+    chip = swap(own, "tensor", 1)
+    core = swap(own, "tensor", 0)
+    return own, core, chip, swap(chip, "tensor", 0)
+
+
+def gather_into(mark, parts, whole):
+    share = parts[0].shape[0]
+    for at, part in enumerate(parts):
+        core = mark[CORE] if at % 2 == 0 else 1 - mark[CORE]
+        chip = mark[CHIP] if at < 2 else 1 - mark[CHIP]
+        first = pl.multiple_of((2 * chip + core) * share, share)
+        whole[pl.ds(first, share), :] = part[...]
+
+
+def hidden_back(marks, cotangent, weight, after=()):
+    rows, full = cotangent.shape
+    inner = weight.shape[0]
+    block = min(256, rows)
+
+    def kernel(mark, c_ref, w_ref, o_ref):
+        o_ref[...] = over_columns(c_ref[...], w_ref[...]).astype(BF16)
+
+    return call(
+        "hidden_back", kernel, marks, (rows // block,), [cotangent, weight],
+        [pl.BlockSpec((block, full), lambda i, mark: (i, 0)), fixed(inner, full)],
+        shape((rows, inner), BF16), pl.BlockSpec((block, inner), lambda i, mark: (i, 0)), after,
+        flops=2 * rows * full * inner, moved=2 * (rows * full + inner * full + rows * inner),
+    )
+
+
+def gate_up(marks, parts, weight, hidden_grad, after=()):
+    share, full = parts[0].shape
+    rows = 4 * share
+    inner = weight.shape[2]
+    tile = 128
+    block = min(256, rows)
+
+    def kernel(mark, p0, p1, p2, p3, w_ref, h_ref, second, hidden, hidden_t, gate_grad, up_grad):
+        @pl.when(pl.program_id(0) == 0)
+        def _():
+            gather_into(mark, (p0, p1, p2, p3), second)
+
+        both = jnp.concatenate([w_ref[0], w_ref[1]], axis=1)
+        for first in range(0, rows, block):
+            at = pl.ds(first, block)
+            got = jnp.dot(second[at, :], both, preferred_element_type=F32)
+            gate, up = got[:, :tile], got[:, tile:]
+            sigmoid = 1.0 / (1.0 + jnp.exp(-gate))
+            active = gate * sigmoid
+            made = (active * up).astype(BF16)
+            hidden[at, :] = made
+            hidden_t[:, at] = made.T
+            grad = h_ref[at, :].astype(F32)
+            gate_grad[at, :] = (grad * up * (sigmoid * (1.0 + gate * (1.0 - sigmoid)))).astype(BF16)
+            up_grad[at, :] = (grad * active).astype(BF16)
+
+    column = pl.BlockSpec((rows, tile), lambda i, mark: (0, i))
+    return call(
+        "gate_up", kernel, marks, (inner // tile,), [*parts, weight, hidden_grad],
+        [fixed(share, full)] * 4 + [pl.BlockSpec((2, full, tile), lambda i, mark: (0, 0, i)), column],
+        [
+            shape((rows, full), BF16), shape((rows, inner), BF16), shape((inner, rows), BF16),
+            shape((rows, inner), BF16), shape((rows, inner), BF16),
+        ],
+        [fixed(rows, full), column, pl.BlockSpec((tile, rows), lambda i, mark: (i, 0)), column, column],
+        after,
+        flops=4 * rows * full * inner, moved=2 * (4 * full * inner + 2 * rows * full + 5 * rows * inner),
+    )
+
+
+def heads_back(marks, parts, weight, after=()):
+    share, full = parts[0].shape
+    rows = 4 * share
+    width = weight.shape[0]
+
+    def kernel(mark, p0, p1, p2, p3, w_ref, low, grad):
+        @pl.when(pl.program_id(0) == 0)
+        def _():
+            gather_into(mark, (p0, p1, p2, p3), low)
+
+        at = pl.ds(pl.multiple_of(pl.program_id(0) * share, share), share)
+        grad[...] = over_columns(low[at, :], w_ref[...]).astype(BF16)
+
+    return call(
+        "heads_back", kernel, marks, (4,), [*parts, weight], [fixed(share, full)] * 4 + [fixed(width, full)],
+        [shape((rows, full), BF16), shape((rows, width), BF16)],
+        [fixed(rows, full), pl.BlockSpec((share, width), lambda i, mark: (i, 0))], after,
+        flops=2 * rows * full * width, moved=2 * (2 * rows * full + full * width + rows * width),
+    )
+
+
+def bit_of(mark, bit):
+    return (mark[DP] >> bit) & 1
+
+
+def block_at(mark, order, flips, j):
+    rest = len(order) - len(flips)
+    index = 0
+    for at, bit in enumerate(order):
+        if at < len(flips):
+            value = bit_of(mark, bit)
+            value = 1 - value if flips[at] else value
+        else:
+            value = (j >> (rest - 1 - (at - len(flips)))) & 1
+        index = index + (value << bit)
+    return index
+
+
+def weight_send(marks, order, columns, other, turned_out, after=()):
+    size = lax.axis_size("dp")
+    rows, full = columns.shape
+    block = full // size
+    count = size // 2
+    dims = (other.shape[0], block) if turned_out else (block, other.shape[1])
+
+    def kernel(mark, c_ref, o_ref, out):
+        if turned_out:
+            got = jnp.dot(o_ref[...], c_ref[...], preferred_element_type=F32)
+        else:
+            got = over_rows(c_ref[...], o_ref[...])
+        out[0] = got.astype(BF16)
+
+    return call(
+        "weight_send", kernel, marks, (count,), [columns, other],
+        [
+            pl.BlockSpec((rows, block), lambda j, mark: (0, block_at(mark, order, (True,), j))),
+            fixed(*other.shape),
+        ],
+        shape((count, *dims), BF16), pl.BlockSpec((1, *dims), lambda j, mark: (j, 0, 0)), after,
+        flops=2 * rows * dims[0] * dims[1] * count,
+        moved=rows * full + 2 * other.size + 2 * count * dims[0] * dims[1],
+    )
+
+
+def weight_keep(marks, order, columns, other, turned_out, arrived, after=()):
+    size = lax.axis_size("dp")
+    rows, full = columns.shape
+    block = full // size
+    half = size // 4
+    dims = (other.shape[0], block) if turned_out else (block, other.shape[1])
+
+    def kernel(mark, c_ref, o_ref, a_ref, send, keep):
+        if turned_out:
+            got = jnp.dot(o_ref[...], c_ref[...], preferred_element_type=F32)
+        else:
+            got = over_rows(c_ref[...], o_ref[...])
+        got = got + a_ref[0].astype(F32)
+
+        @pl.when(pl.program_id(0) < half)
+        def _():
+            send[0] = got.astype(BF16)
+
+        @pl.when(pl.program_id(0) >= half)
+        def _():
+            keep[0] = got
+
+    def block_for(j, mark):
+        away = block_at(mark, order, (False, True), j)
+        here = block_at(mark, order, (False, False), j - half)
+        return jnp.where(j < half, away, here)
+
+    def arrived_for(j, mark):
+        mine = bit_of(mark, order[1])
+        return jnp.where(j < half, (1 - mine) * half + j, mine * half + j - half)
+
+    return call(
+        "weight_keep", kernel, marks, (2 * half,), [columns, other, arrived],
+        [
+            pl.BlockSpec((rows, block), lambda j, mark: (0, block_for(j, mark))),
+            fixed(*other.shape),
+            pl.BlockSpec((1, *dims), lambda j, mark: (arrived_for(j, mark), 0, 0)),
+        ],
+        [shape((half, *dims), BF16), shape((half, *dims), F32)],
+        [
+            pl.BlockSpec((1, *dims), lambda j, mark: (jnp.minimum(j, half - 1), 0, 0)),
+            pl.BlockSpec((1, *dims), lambda j, mark: (jnp.maximum(j - half, 0), 0, 0)),
+        ],
+        after,
+        flops=2 * rows * dims[0] * dims[1] * 2 * half,
+        moved=rows * full + 2 * other.size + 8 * half * dims[0] * dims[1],
+    )
+
+
+def finish(order, keep, arrived):
+    me = lax.axis_index("dp")
+    total = keep + arrived.astype(F32)
+    for bit in order[2:]:
         mine = (me >> bit) & 1
-        total = total.reshape(-1, 2, *total.shape[1:])
-        arrived = swap(pick(total, 1 - mine, 1).astype(BF16), "tensor", bit)
-        total = pick(total, mine, 1) + arrived.astype(F32)
+        total = total.reshape(2, -1, *total.shape[1:])
+        arrived = swap(pick(total, 1 - mine, 0).astype(BF16), "dp", bit)
+        total = pick(total, mine, 0) + arrived.astype(F32)
     return total[0]
 
 
-def spread_rows(own):
-    size = lax.axis_size("tensor")
-    me = lax.axis_index("tensor")
-    bits = size.bit_length() - 1
-    rows, columns = own.shape
-    held = own[None]
-    for bit in reversed(range(bits)):
-        other = swap(held, "tensor", bit)
-        mine = ((me >> bit) & 1) == 0
-        held = jnp.stack([jnp.where(mine, held, other), jnp.where(mine, other, held)], axis=1)
-        held = held.reshape(-1, rows, columns)
-    return held.reshape(-1, columns)
-
-
-def sum_parts(send, keep, shape_back):
-    size = lax.axis_size("dp")
-    me = lax.axis_index("dp")
-    bits = size.bit_length() - 1
-    arrived = swap(send, "dp", 0)
-    total = keep + arrived.astype(F32)
-    for bit in range(1, bits):
-        mine = (me >> bit) & 1
-        total = total.reshape(-1, 2, *total.shape[1:])
-        arrived = swap(pick(total, 1 - mine, 1).astype(BF16), "dp", bit)
-        total = pick(total, mine, 1) + arrived.astype(F32)
-    return total[0]
-
-
-def halves(values):
-    size = lax.axis_size("dp")
-    me = lax.axis_index("dp") & 1
-    cut = values.reshape(values.shape[0], size // 2, 2, values.shape[1] // size)
-    return pick(cut, 1 - me, 2), pick(cut, me, 2)
+def plain_weight(columns, other, turned_out):
+    if turned_out:
+        got = jnp.einsum("fr,rd->fd", other, columns, preferred_element_type=F32)
+    else:
+        got = jnp.einsum("rd,rf->df", columns, other, preferred_element_type=F32)
+    return lax.psum_scatter(
+        got.astype(BF16), "dp", scatter_dimension=1 if turned_out else 0, tiled=True
+    ).astype(F32)
+
+
+def everywhere(values):
+    for axis in ("dp", "tensor"):
+        for bit in range(lax.axis_size(axis).bit_length() - 1):
+            values = values + swap(values, axis, bit)
+    return values
 
 
 def body(
@@ -340,117 +624,112 @@
     cotangent,
 ):
     row_count, full_width = tokens.shape
-    share = row_count // lax.axis_size("tensor")
-    first_row = lax.axis_index("tensor") * share
     local_width = qkv_weight.shape[2]
-
-    def own_rows(values):
-        return lax.dynamic_slice_in_dim(values, first_row, share, 0)
+    tensor_at, dp_at, dp_size = lax.axis_index("tensor"), lax.axis_index("dp"), lax.axis_size("dp")
+    marks = jnp.stack([tensor_at & 1, tensor_at >> 1, dp_at]).astype(jnp.int32)
+    bits = dp_size.bit_length() - 1
+    x_first = tuple(range(bits))
+    z_first = (1, 0) + x_first[2:]
+    fine = (full_width // dp_size) % 128 == 0
+
+    def send(order, columns, other, turned_out, after):
+        if not fine:
+            return columns
+        return weight_send(marks, order, columns, other, turned_out, after)
+
+    def keep(order, columns, other, turned_out, sent, after):
+        if not fine:
+            return columns, None
+        return weight_keep(
+            marks, order, columns, other, turned_out, swap(sent, "dp", order[0]), after
+        )
+
+    def total(order, columns, other, turned_out, kept):
+        if not fine:
+            return plain_weight(columns, other, turned_out)
+        return finish(order, kept[1], swap(kept[0], "dp", order[1]))
 
     begins, *tables = positions(seq_lengths[0], row_count)
     normed, queries, keys, values = project(
         tokens, qkv_weight, qkv_bias, norm_gains[0], norm_shifts[0], tables
     )
     heads_out, logs = attend(begins, queries, keys, values)
-    inputs_own = own_rows(tokens).astype(F32)
-    cotangent_own = own_rows(cotangent).astype(F32)
-    residual_own = inputs_own + sum_rows(heads_out, lambda left: dot(left, out_weight))
-    unit_second, inverse_second = norm_parts(residual_own)
-    second = spread_rows((unit_second * norm_gains[1] + norm_shifts[1]).astype(BF16))
-    gate = dot(second, gate_up_weight[0])
-    upper = dot(second, gate_up_weight[1])
-    hidden_grad = jnp.einsum("td,fd->tf", cotangent, down_weight, preferred_element_type=F32)
-    sigmoid_gate = jax.nn.sigmoid(gate)
-    activated = gate * sigmoid_gate
-    hidden = (activated * upper).astype(BF16)
-    gate_grad = (
-        hidden_grad * upper * (sigmoid_gate * (1.0 + gate * (1.0 - sigmoid_gate)))
+    sent = rows_product(marks, [heads_out], out_weight, False)
+    to_chip, own = rows_product(marks, [heads_out], out_weight, False, swap(sent, "tensor", 0))
+    hidden_grad = hidden_back(marks, cotangent, down_weight, [own])
+    residual, second_own = norm_rows(
+        marks, tokens, own, swap(to_chip, "tensor", 1), norm_gains[1], norm_shifts[1], [hidden_grad]
+    )
+    second, hidden, hidden_t, gate_grad, up_grad = gate_up(
+        marks, spread(second_own), gate_up_weight, hidden_grad
+    )
+    down_sent = send(x_first, cotangent, hidden_t, True, [])
+    second_sent = rows_product(marks, [gate_grad, up_grad], gate_up_weight, True, None, [down_sent])
+    up_sent = send(x_first, second, up_grad, False, [second_sent])
+    to_chip, own = rows_product(
+        marks, [gate_grad, up_grad], gate_up_weight, True, swap(second_sent, "tensor", 0), [up_sent]
+    )
+    gate_sent = send(z_first, second, gate_grad, False, [own])
+    branch_sent = rows_product(marks, [hidden], down_weight, False, None, [gate_sent])
+    branch_to_chip, branch_own = rows_product(
+        marks, [hidden], down_weight, False, swap(branch_sent, "tensor", 0), [gate_sent]
+    )
+    residual_grad, residual_low_own, second_sums = norm_back_rows(
+        marks, residual, cotangent, own, swap(to_chip, "tensor", 1), norm_gains[1], [branch_own]
+    )
+    block_out = (
+        residual + branch_own + swap(branch_to_chip, "tensor", 1).astype(F32)
     ).astype(BF16)
-    upper_grad = (hidden_grad * activated).astype(BF16)
-
-    cotangent_send, cotangent_keep = halves(cotangent)
-    down_part = sum_parts(
-        jnp.einsum("tf,tbc->bfc", hidden, cotangent_send, preferred_element_type=F32).astype(BF16),
-        jnp.einsum("tf,tbc->bfc", hidden, cotangent_keep, preferred_element_type=F32),
-        None,
-    )
-    second_send, second_keep = halves(second)
-
-    def weight_part(send, keep, grads):
-        return sum_parts(
-            jnp.einsum("tbd,tf->bdf", send, grads, preferred_element_type=F32).astype(BF16),
-            jnp.einsum("tbd,tf->bdf", keep, grads, preferred_element_type=F32),
-            None,
-        )
-
-    gate_up_part = jnp.stack(
-        [
-            weight_part(second_send, second_keep, gate_grad),
-            weight_part(second_send, second_keep, upper_grad),
-        ]
-    )
-    branch_own = sum_rows(hidden, lambda left: dot(left, down_weight))
-    block_out = (residual_own + branch_own).astype(BF16)
-
-    def second_back(left):
-        gates, uppers = jnp.split(left, 2, axis=1)
-        return jnp.einsum(
-            "tf,df->td", gates, gate_up_weight[0], preferred_element_type=F32
-        ) + jnp.einsum("tf,df->td", uppers, gate_up_weight[1], preferred_element_type=F32)
-
-    second_grad_own = sum_rows(jnp.concatenate([gate_grad, upper_grad], axis=1), second_back)
-    residual_grad_own = cotangent_own + norm_back(
-        unit_second, inverse_second, norm_gains[1], second_grad_own
-    )
-    residual_low = spread_rows(residual_grad_own.astype(BF16))
-    gain_second = jnp.sum(second_grad_own * unit_second, axis=0)
-    shift_second = jnp.sum(second_grad_own, axis=0)
-    heads_grad = jnp.einsum(
-        "td,ed->te", residual_low, out_weight, preferred_element_type=F32
-    ).astype(BF16)
-    low_send, low_keep = halves(residual_low)
-    out_part = sum_parts(
-        jnp.einsum("tf,tbc->bfc", heads_out, low_send, preferred_element_type=F32).astype(BF16),
-        jnp.einsum("tf,tbc->bfc", heads_out, low_keep, preferred_element_type=F32),
-        None,
-    )
+    down_kept = keep(x_first, cotangent, hidden_t, True, down_sent, [residual_low_own])
+    residual_low, heads_grad = heads_back(
+        marks, spread(residual_low_own), out_weight, [down_kept[0]]
+    )
+    heads_t = heads_out.T
+    out_sent = send(x_first, residual_low, heads_t, True, [heads_grad])
     projected_low = attend_back(begins, queries, keys, values, heads_grad, logs, tables)
-    normed_send, normed_keep = halves(normed)
-    qkv_part = jnp.stack([weight_part(normed_send, normed_keep, g) for g in projected_low])
+    gate_kept = keep(z_first, second, gate_grad, False, gate_sent, [projected_low[0]])
+    qkv_sent = []
+    before = gate_kept[0]
+    for grads in projected_low:
+        before = send(x_first, normed, grads, False, [before])
+        qkv_sent.append(before)
+    normed_sent = rows_product(marks, projected_low, qkv_weight, True, None, [before])
+    up_kept = keep(x_first, second, up_grad, False, up_sent, [normed_sent])
+    to_chip, own = rows_product(
+        marks, projected_low, qkv_weight, True, swap(normed_sent, "tensor", 0), [normed_sent]
+    )
+    input_grad, _, first_sums = norm_back_rows(
+        marks, tokens, residual_grad, own, swap(to_chip, "tensor", 1), norm_gains[0], [up_kept[0]]
+    )
     bias_local = jnp.stack([jnp.sum(g, axis=0, dtype=F32) for g in projected_low])
-
-    def normed_back(left):
-        return sum(
-            jnp.einsum("te,de->td", piece, qkv_weight[j], preferred_element_type=F32)
-            for j, piece in enumerate(jnp.split(left, 3, axis=1))
-        )
-
-    normed_grad_own = sum_rows(jnp.concatenate(projected_low, axis=1), normed_back)
-    unit_first, inverse_first = norm_parts(inputs_own)
-    input_grad = residual_grad_own + norm_back(
-        unit_first, inverse_first, norm_gains[0], normed_grad_own
-    )
-    gain_first = jnp.sum(normed_grad_own * unit_first, axis=0)
-    shift_first = jnp.sum(normed_grad_own, axis=0)
     bias_placed = lax.dynamic_update_slice(
-        jnp.zeros((3, full_width), F32),
-        bias_local,
-        (0, lax.axis_index("tensor") * local_width),
-    )
-    gains_grad, shifts_grad, bias_grad = lax.psum(
-        (jnp.stack([gain_first, gain_second]), jnp.stack([shift_first, shift_second]), bias_placed),
-        ("dp", "tensor"),
-    )
+        jnp.zeros((3, full_width), F32), bias_local, (0, tensor_at * local_width)
+    )
+    sums = everywhere(jnp.concatenate([first_sums, second_sums, bias_placed], axis=0))
+    out_kept = keep(x_first, residual_low, heads_t, True, out_sent, [input_grad])
+    qkv_kept = []
+    before = out_kept[0]
+    for grads, sent in zip(projected_low, qkv_sent):
+        kept = keep(x_first, normed, grads, False, sent, [before])
+        before = kept[0]
+        qkv_kept.append(kept)
     return (
         block_out,
         input_grad,
-        qkv_part,
-        bias_grad,
-        out_part,
-        gate_up_part,
-        down_part,
-        gains_grad,
-        shifts_grad,
+        jnp.stack(
+            [total(x_first, normed, g, False, k) for g, k in zip(projected_low, qkv_kept)]
+        ),
+        sums[4:7],
+        total(x_first, residual_low, heads_t, True, out_kept),
+        jnp.stack(
+            [
+                total(z_first, second, gate_grad, False, gate_kept),
+                total(x_first, second, up_grad, False, up_kept),
+            ]
+        ),
+        total(x_first, cotangent, hidden_t, True, down_kept),
+        jnp.stack([sums[0], sums[2]]),
+        jnp.stack([sums[1], sums[3]]),
     )
 
 

time: 859 us -> 627 us (0.73)
  Pallas kernels: 62.4 us -> 302 us
  local copies, waits for them, and re-layouts: 192 us -> 14.3 us
  matrix products: 165 us -> 0 us
  waiting for transfers between devices: 300 us -> 236 us
  blocking collectives: 41.7 us -> 0 us
  other arithmetic: 47.3 us -> 29.4 us
    pallas_call x3 -> x31, Pallas kernels: 62.4 us -> 302 us  [the longest x28 240 us: call(): pl.pallas_call(inner, grid_spec=pltpu.PrefetchScalarGridSpec(num_scalar_p...]
    dot_general x32 -> x0, matrix products: 165 us -> none  [the longest x6 46.2 us: dot(): return jnp.dot(left, right, preferred_element_type=F32)]
    dynamic_slice x18 -> x0, local copies, waits for them, and re-layouts: 116 us -> none  [pick(): return lax.dynamic_index_in_dim(values, at, axis, keepdims=False)]
    ppermute x33 -> x40, waiting for transfers between devices: 300 us -> 236 us  [swap(): return lax.ppermute(values, axis, [(i, i ^ 1 << bit) for i in range(size)])]
    psum x1 -> x0, blocking collectives: 41.7 us -> none  [body(): lax.psum((jnp.stack([gain_first, gain_second]), jnp.stack([shift_first, s...]
    unnamed x112 -> x50, local copies, waits for them, and re-layouts: 35.8 us -> 8.72 us
    another operation x4 -> x0, local copies, waits for them, and re-layouts: 20.3 us -> none  [the longest x2 15.7 us: halves(): cut = values.reshape(values.shape[0], size // 2, 2, values.shape[1] // size)]
    reshape x2 -> x0, local copies, waits for them, and re-layouts: 15.6 us -> none  [halves(): cut = values.reshape(values.shape[0], size // 2, 2, values.shape[1] // size)]
  transfers between devices with their start and end apart: 33 -> 40, of which waited for: 15 -> 19; matrix products, arithmetic and copies ran while one was open for 26% -> 4% of each run, Pallas kernels for 0% -> 28%
where the time goes in v2:
time: 627 us; the launch traced here: 623 us
  Pallas kernels  302 us (48%)
  waiting for transfers between devices  236 us (38%)
  starting transfers between devices  41.3 us (7%)
  other arithmetic  29.4 us (5%)
  local copies, waits for them, and re-layouts  14.3 us (2%)
    pallas_call x28, Pallas kernels, call(): pl.pallas_call(inner, grid_spec=pltpu.PrefetchScalarGridSpec(num_scalar_p...  240 us
    ppermute x40, waiting for transfers between devices, swap(): return lax.ppermute(values, axis, [(i, i ^ 1 << bit) for i in range(size)])  236 us
    ppermute x40, starting transfers between devices, swap(): return lax.ppermute(values, axis, [(i, i ^ 1 << bit) for i in range(size)])  41.3 us
    pallas_call x1, Pallas kernels, attend_back(): pl.pallas_call(functools.partial(attend_back_kernel, blocks), name='atten...  28.4 us
    pallas_call x1, Pallas kernels, attend(): pl.pallas_call(functools.partial(attend_kernel, blocks), name='attend', g...  20.2 us
    pallas_call x1, Pallas kernels, project(): pl.pallas_call(qkv_kernel, name='project', grid=(rows // block,), in_spec...  13.9 us
  transfers between devices with their start and end apart: 40, of which 19 were waited for; matrix products, arithmetic and copies ran while one was open for 4% of the time, Pallas kernels for 28%

profile of v2, /device:TPU:0, one launch (start us, length us, event | category | flops | bytes accessed | tf_op | source)
XLA Modules:
  0.0 623.5 jit_solution(12391527100511791323)
XLA Ops:
  8.7 13.9 %project.1 = (bf16[1024,2048]{1,0:T(8,128)(2,1)}, bf16[1024,512]{1,0:T(8,128)(2,1)}, bf16[1024,512]{1,0:T(8,128)(2,1)}, bf16[1024,512]{1,0:T(8,128)(2,1)}) custom-call(bf16[1024,2048]{1,0:T(8,128)(2,1)} %refs_0_.9, bf16[3,2048,512]{2,1,0:T(8,128)(2,1)} %refs_3_.3, f32[3,512]{1,0:T(4,128)} %convert_element_type.109.b_ref, ...), custom_call_target="tpu_custom_call" | custom-call | tf_op jit(solution)/shard_map/project/pallas_call | solution.py:90
  22.6 20.2 %attend.1 = (bf16[1024,512]{1,0:T(8,128)(2,1)}, f32[8,1,1024]{2,1,0:T(1,128)}) custom-call(s32[1,1024]{1,0:T(1,128)} %bitcast.36, bf16[1024,512]{1,0:T(8,128)(2,1)} %get-tuple-element.54.q_ref, bf16[1024,512]{1,0:T(8,128)(2,1)} %get-tuple-element.55.k_ref, bf16[1024,512]{1,0:T(8,128)(2,1)} %get-tuple-element.56.v_ref), custom_call_target="tpu_custom_call" | custom-call | tf_op jit(solution)/shard_map/attend/pallas_call | solution.py:163
  42.7 7.5 %rows_send.4 = bf16[2,256,2048]{2,1,0:T(8,128)(2,1)} custom-call(s32[3]{0:T(128)} %pad_add_fusion.mark, bf16[2,2,256,512]{3,2,1,0:T(8,128)(2,1)} %bitcast.34, bf16[512,2048]{1,0:T(8,128)(2,1)} %refs_4_.3), custom_call_target="tpu_custom_call" | custom-call | tf_op jit(solution)/shard_map/rows_send/pallas_call | solution.py:263
  50.7 4.0 collective-permute-done.refs_2_
  56.0 8.1 %rows_keep.4 = (bf16[256,2048]{1,0:T(8,128)(2,1)}, f32[256,2048]{1,0:T(8,128)}) custom-call(s32[3]{0:T(128)} %pad_add_fusion.mark, bf16[2,2,256,512]{3,2,1,0:T(8,128)(2,1)} %bitcast.35, bf16[512,2048]{1,0:T(8,128)(2,1)} %refs_4_.3, bf16[2,256,2048]{2,1,0:T(8,128)(2,1)} %copy-done.11), custom_call_target="tpu_custom_call" | custom-call | tf_op jit(solution)/shard_map/rows_keep/pallas_call | solution.py:263
  67.0 11.8 %hidden_back.1.refs_5_ = bf16[1024,1408]{1,0:T(8,128)(2,1)} custom-call(s32[3]{0:T(128)} %pad_add_fusion.mark, bf16[1024,2048]{1,0:T(8,128)(2,1)} %refs_0_.8, bf16[1408,2048]{1,0:T(8,128)(2,1)} %refs_1_.10, f32[256,2048]{1,0:T(8,128)} %get-tuple-element.58.refs_2_.refs_1_), custom_call_target="tpu_custom_call" | custom-call | tf_op jit(solution)/shard_map/hidden_back/pallas_call | solution.py:263
  78.8 11.8 %collective-permute-done.1.refs_2_ = bf16[256,2048]{1,0:T(8,128)(2,1)S(1)} collective-permute-done((bf16[256,2048]{1,0:T(8,128)(2,1)}, bf16[256,2048]{1,0:T(8,128)(2,1)S(1)}, u32[]{:S(2)}, u32[]{:S(2)}) %collective-permute-start.1) | collective-permute-done | bytes 1048608 | tf_op jit(solution)/shard_map/ppermute | solution.py:293
  91.6 4.2 norm_rows.1
  97.6 23.1 %collective-permute-done.3.refs_2_ = bf16[256,2048]{1,0:T(8,128)(2,1)S(1)} collective-permute-done((bf16[256,2048]{1,0:T(8,128)(2,1)}, bf16[256,2048]{1,0:T(8,128)(2,1)S(1)}, u32[]{:S(2)}, u32[]{:S(2)}) %collective-permute-start.3) | collective-permute-done | bytes 1048608 | tf_op jit(solution)/shard_map/ppermute | solution.py:293
  124.4 23.0 %gate_up.1 = (bf16[1024,2048]{1,0:T(8,128)(2,1)}, bf16[1024,1408]{1,0:T(8,128)(2,1)}, bf16[1408,1024]{1,0:T(8,128)(2,1)}, bf16[1024,1408]{1,0:T(8,128)(2,1)}, bf16[1024,1408]{1,0:T(8,128)(2,1)}) custom-call(s32[3]{0:T(128)} %pad_add_fusion.mark, bf16[256,2048]{1,0:T(8,128)(2,1)} %get-tuple-element.61.refs_0_, bf16[256,2048]{1,0:T(8,128)(2,1)} %copy-done.20, ...), custom_call_target="tpu_custom_call" | custom-call | tf_op jit(solution)/shard_map/gate_up/pallas_call | solution.py:263
  147.4 7.7 %weight_send.7.refs_3_ = bf16[4,1408,256]{2,1,0:T(8,128)(2,1)} custom-call(s32[3]{0:T(128)} %pad_add_fusion.mark, bf16[1024,2048]{1,0:T(8,128)(2,1)} %refs_0_.8, bf16[1408,1024]{1,0:T(8,128)(2,1)} %get-tuple-element.66.refs_1_), custom_call_target="tpu_custom_call" | custom-call | tf_op jit(solution)/shard_map/weight_send/pallas_call | solution.py:263
  155.0 13.3 %rows_send.5.refs_2_ = bf16[2,256,2048]{2,1,0:T(8,128)(2,1)} custom-call(s32[3]{0:T(128)} %pad_add_fusion.mark, bf16[2,2,256,1408]{3,2,1,0:T(8,128)(2,1)} %bitcast.22, bf16[2,2,256,1408]{3,2,1,0:T(8,128)(2,1)} %bitcast.20, bf16[2,2048,1408]{2,1,0:T(8,128)(2,1)} %refs_2_.3, bf16[4,1408,256]{2,1,0:T(8,128)(2,1)} %weight_send.7.refs_3_), custom_call_target="tpu_custom_call" | custom-call | tf_op jit(solution)/shard_map/rows_send/pallas_call | solution.py:263
  168.5 8.0 %weight_send.8.refs_4_ = bf16[4,256,1408]{2,1,0:T(8,128)(2,1)} custom-call(s32[3]{0:T(128)} %pad_add_fusion.mark, bf16[1024,2048]{1,0:T(8,128)(2,1)} %get-tuple-element.63.refs_0_, bf16[1024,1408]{1,0:T(8,128)(2,1)} %get-tuple-element.65.refs_1_, bf16[2,256,2048]{2,1,0:T(8,128)(2,1)} %rows_send.5.refs_2_), custom_call_target="tpu_custom_call" | custom-call | tf_op jit(solution)/shard_map/weight_send/pallas_call | solution.py:263
  177.8 14.0 %rows_keep.5 = (bf16[256,2048]{1,0:T(8,128)(2,1)}, f32[256,2048]{1,0:T(8,128)}) custom-call(s32[3]{0:T(128)} %pad_add_fusion.mark, bf16[2,2,256,1408]{3,2,1,0:T(8,128)(2,1)} %bitcast.23, bf16[2,2,256,1408]{3,2,1,0:T(8,128)(2,1)} %bitcast.21, bf16[2,2048,1408]{2,1,0:T(8,128)(2,1)} %refs_2_.3, bf16[2,256,2048]{2,1,0:T(8,128)(2,1)} %copy-done.10, ...), custom_call_target="tpu_custom_call" | custom-call | tf_op jit(solution)/shard_map/rows_keep/pallas_call | solution.py:263
  191.8 8.0 %weight_send.9.refs_2_.refs_3_ = bf16[4,256,1408]{2,1,0:T(8,128)(2,1)} custom-call(s32[3]{0:T(128)} %pad_add_fusion.mark, bf16[1024,2048]{1,0:T(8,128)(2,1)} %get-tuple-element.63.refs_0_, bf16[1024,1408]{1,0:T(8,128)(2,1)} %get-tuple-element.64.refs_1_, f32[256,2048]{1,0:T(8,128)} %get-tuple-element.67.refs_2_), custom_call_target="tpu_custom_call" | custom-call | tf_op jit(solution)/shard_map/weight_send/pallas_call | solution.py:263
  199.8 10.0 %rows_send.6 = bf16[2,256,2048]{2,1,0:T(8,128)(2,1)} custom-call(s32[3]{0:T(128)} %pad_add_fusion.mark, bf16[2,2,256,1408]{3,2,1,0:T(8,128)(2,1)} %bitcast.30, bf16[1408,2048]{1,0:T(8,128)(2,1)} %refs_1_.10, bf16[4,256,1408]{2,1,0:T(8,128)(2,1)} %weight_send.9.refs_2_.refs_3_), custom_call_target="tpu_custom_call" | custom-call | tf_op jit(solution)/shard_map/rows_send/pallas_call | solution.py:263
  214.7 10.3 %rows_keep.6 = (bf16[256,2048]{1,0:T(8,128)(2,1)}, f32[256,2048]{1,0:T(8,128)}) custom-call(s32[3]{0:T(128)} %pad_add_fusion.mark, bf16[2,2,256,1408]{3,2,1,0:T(8,128)(2,1)} %bitcast.31, bf16[1408,2048]{1,0:T(8,128)(2,1)} %refs_1_.10, bf16[2,256,2048]{2,1,0:T(8,128)(2,1)} %collective-permute-done.6.refs_2_, bf16[4,256,1408]{2,1,0:T(8,128)(2,1)} %weight_send.9.refs_2_.refs_3_), custom_call_target="tpu_custom_call" | custom-call | tf_op jit(solution)/shard_map/rows_keep/pallas_call | solution.py:263
  225.0 11.7 %collective-permute-done.8.refs_3_ = bf16[256,2048]{1,0:T(8,128)(2,1)S(1)} collective-permute-done((bf16[256,2048]{1,0:T(8,128)(2,1)}, bf16[256,2048]{1,0:T(8,128)(2,1)S(1)}, u32[]{:S(2)}, u32[]{:S(2)}) %collective-permute-start.8) | collective-permute-done | bytes 1048608 | tf_op jit(solution)/shard_map/ppermute | solution.py:293
  237.7 5.5 norm_back_rows.2
  245.2 22.3 %collective-permute-done.10.refs_2_ = bf16[256,2048]{1,0:T(8,128)(2,1)S(1)} collective-permute-done((bf16[256,2048]{1,0:T(8,128)(2,1)}, bf16[256,2048]{1,0:T(8,128)(2,1)S(1)}, u32[]{:S(2)}, u32[]{:S(2)}) %collective-permute-start.10) | collective-permute-done | bytes 1048608 | tf_op jit(solution)/shard_map/ppermute | solution.py:293
  267.6 8.2 %collective-permute-done.12.refs_2_ = bf16[4,1408,256]{2,1,0:T(8,128)(2,1)} collective-permute-done((bf16[4,1408,256]{2,1,0:T(8,128)(2,1)}, bf16[4,1408,256]{2,1,0:T(8,128)(2,1)}, u32[]{:S(2)}, u32[]{:S(2)}) %collective-permute-start.12) | collective-permute-done | bytes 2883616 | tf_op jit(solution)/shard_map/ppermute | solution.py:293
  277.2 8.9 %weight_keep.7 = (bf16[2,1408,256]{2,1,0:T(8,128)(2,1)}, f32[2,1408,256]{2,1,0:T(8,128)}) custom-call(s32[3]{0:T(128)} %pad_add_fusion.mark, bf16[1024,2048]{1,0:T(8,128)(2,1)} %refs_0_.8, bf16[1408,1024]{1,0:T(8,128)(2,1)} %get-tuple-element.66.refs_1_, bf16[4,1408,256]{2,1,0:T(8,128)(2,1)} %collective-permute-done.12.refs_2_, ...), custom_call_target="tpu_custom_call" | custom-call | tf_op jit(solution)/shard_map/weight_keep/pallas_call | solution.py:263
  287.8 8.3 %heads_back.1 = (bf16[1024,2048]{1,0:T(8,128)(2,1)}, bf16[1024,512]{1,0:T(8,128)(2,1)}) custom-call(s32[3]{0:T(128)} %pad_add_fusion.mark, bf16[256,2048]{1,0:T(8,128)(2,1)} %get-tuple-element.72.refs_3_.refs_0_, bf16[256,2048]{1,0:T(8,128)(2,1)} %collective-permute-done.9.refs_1_, bf16[256,2048]{1,0:T(8,128)(2,1)} %copy-done.17, ...), custom_call_target="tpu_custom_call" | custom-call | tf_op jit(solution)/shard_map/heads_back/pallas_call | solution.py:263
  296.1 28.4 %attend_back.1 = (bf16[1024,512]{1,0:T(8,128)(2,1)}, bf16[1024,512]{1,0:T(8,128)(2,1)}, bf16[1024,512]{1,0:T(8,128)(2,1)}) custom-call(s32[1,1024]{1,0:T(1,128)} %bitcast.37, bf16[1024,512]{1,0:T(8,128)(2,1)} %get-tuple-element.54.q_ref, bf16[1024,512]{1,0:T(8,128)(2,1)} %get-tuple-element.55.k_ref, bf16[1024,512]{1,0:T(8,128)(2,1)} %get-tuple-element.56.v_ref, ...), custom_call_target="tpu_custom_call" | custom-call | tf_op jit(solution)/shard_map/attend_back/pallas_call | solution.py:232
  324.5 9.2 %weight_keep.8 = (bf16[2,256,1408]{2,1,0:T(8,128)(2,1)}, f32[2,256,1408]{2,1,0:T(8,128)}) custom-call(s32[3]{0:T(128)} %pad_add_fusion.mark, bf16[1024,2048]{1,0:T(8,128)(2,1)} %get-tuple-element.63.refs_0_, bf16[1024,1408]{1,0:T(8,128)(2,1)} %get-tuple-element.64.refs_1_, bf16[4,256,1408]{2,1,0:T(8,128)(2,1)} %collective-permute-done.13.refs_2_, ...), custom_call_target="tpu_custom_call" | custom-call | tf_op jit(solution)/shard_map/weight_keep/pallas_call | solution.py:263
  333.7 5.5 weight_send.10.refs_2_
  339.2 5.5 weight_send.11.refs_2_
  344.7 5.5 weight_send.12.refs_4_
  350.2 10.4 %rows_send.7.refs_5_.refs_3_ = bf16[2,256,2048]{2,1,0:T(8,128)(2,1)} custom-call(s32[3]{0:T(128)} %pad_add_fusion.mark, bf16[2,2,256,512]{3,2,1,0:T(8,128)(2,1)} %bitcast.24, bf16[2,2,256,512]{3,2,1,0:T(8,128)(2,1)} %bitcast.28, bf16[2,2,256,512]{3,2,1,0:T(8,128)(2,1)} %bitcast.26, bf16[3,2048,512]{2,1,0:T(8,128)(2,1)} %refs_3_.3, ...), custom_call_target="tpu_custom_call" | custom-call | tf_op jit(solution)/shard_map/rows_send/pallas_call | solution.py:263
  362.6 3.6 add_convert_fusion
  375.2 9.2 %weight_keep.9 = (bf16[2,256,1408]{2,1,0:T(8,128)(2,1)}, f32[2,256,1408]{2,1,0:T(8,128)}) custom-call(s32[3]{0:T(128)} %pad_add_fusion.mark, bf16[1024,2048]{1,0:T(8,128)(2,1)} %get-tuple-element.63.refs_0_, bf16[1024,1408]{1,0:T(8,128)(2,1)} %get-tuple-element.65.refs_1_, bf16[4,256,1408]{2,1,0:T(8,128)(2,1)} %collective-permute-done.16.refs_2_, ...), custom_call_target="tpu_custom_call" | custom-call | tf_op jit(solution)/shard_map/weight_keep/pallas_call | solution.py:263
  384.8 5.6 weight_send.13
  391.8 10.5 %rows_keep.7 = (bf16[256,2048]{1,0:T(8,128)(2,1)}, f32[256,2048]{1,0:T(8,128)}) custom-call(s32[3]{0:T(128)} %pad_add_fusion.mark, bf16[2,2,256,512]{3,2,1,0:T(8,128)(2,1)} %bitcast.25, bf16[2,2,256,512]{3,2,1,0:T(8,128)(2,1)} %bitcast.29, bf16[2,2,256,512]{3,2,1,0:T(8,128)(2,1)} %bitcast.27, bf16[3,2048,512]{2,1,0:T(8,128)(2,1)} %refs_3_.3, ...), custom_call_target="tpu_custom_call" | custom-call | tf_op jit(solution)/shard_map/rows_keep/pallas_call | solution.py:263
  407.8 18.6 %collective-permute-done.15.refs_3_ = bf16[256,2048]{1,0:T(8,128)(2,1)} collective-permute-done((bf16[256,2048]{1,0:T(8,128)(2,1)}, bf16[256,2048]{1,0:T(8,128)(2,1)}, u32[]{:S(2)}, u32[]{:S(2)}) %collective-permute-start.15) | collective-permute-done | bytes 1048608 | tf_op jit(solution)/shard_map/ppermute | solution.py:293
  426.7 5.7 norm_back_rows.3
  437.7 8.4 %collective-permute-done.27 = f32[7,2048]{1,0:T(8,128)S(1)} collective-permute-done((f32[7,2048]{1,0:T(8,128)S(1)}, f32[7,2048]{1,0:T(8,128)S(1)}, u32[]{:S(2)}, u32[]{:S(2)}) %collective-permute-start.27) | collective-permute-done | bytes 57376 | tf_op jit(solution)/shard_map/ppermute | solution.py:293
  446.7 13.6 %collective-permute-done.28 = f32[7,2048]{1,0:T(8,128)S(1)} collective-permute-done((f32[7,2048]{1,0:T(8,128)S(1)}, f32[7,2048]{1,0:T(8,128)S(1)}, u32[]{:S(2)}, u32[]{:S(2)}) %collective-permute-start.28) | collective-permute-done | bytes 57376 | tf_op jit(solution)/shard_map/ppermute | solution.py:293
  467.1 29.4 %collective-permute-done.29 = f32[7,2048]{1,0:T(8,128)S(1)} collective-permute-done((f32[7,2048]{1,0:T(8,128)S(1)}, f32[7,2048]{1,0:T(8,128)S(1)}, u32[]{:S(2)}, u32[]{:S(2)}) %collective-permute-start.29) | collective-permute-done | bytes 57376 | tf_op jit(solution)/shard_map/ppermute | solution.py:293
  502.8 18.8 %collective-permute-done.18.refs_2_ = bf16[4,512,256]{2,1,0:T(8,128)(2,1)} collective-permute-done((bf16[4,512,256]{2,1,0:T(8,128)(2,1)S(1)}, bf16[4,512,256]{2,1,0:T(8,128)(2,1)}, u32[]{:S(2)}, u32[]{:S(2)}) %collective-permute-start.18) | collective-permute-done | bytes 1048608 | tf_op jit(solution)/shard_map/ppermute | solution.py:293
  521.6 5.9 weight_keep.10
  527.5 6.0 weight_keep.11
  535.5 6.0 weight_keep.12
  541.6 6.0 weight_keep.13
  551.4 23.0 %collective-permute-done.25 = bf16[2,256,512]{2,1,0:T(8,128)(2,1)S(1)} collective-permute-done((bf16[2,256,512]{2,1,0:T(8,128)(2,1)}, bf16[2,256,512]{2,1,0:T(8,128)(2,1)S(1)}, u32[]{:S(2)}, u32[]{:S(2)}) %collective-permute-start.25) | collective-permute-done | bytes 524320 | tf_op jit(solution)/shard_map/ppermute | solution.py:293
  582.7 23.2 %collective-permute-done.26 = bf16[1,256,512]{2,1,0:T(8,128)(2,1)S(1)} collective-permute-done((bf16[1,256,512]{2,1,0:T(8,128)(2,1)S(1)}, bf16[1,256,512]{2,1,0:T(8,128)(2,1)S(1)}, u32[]{:S(2)}, u32[]{:S(2)}) %collective-permute-start.26) | collective-permute-done | bytes 262176 | tf_op jit(solution)/shard_map/ppermute | solution.py:293
  606.0 5.5 collective-permute-done.23
  611.6 5.5 collective-permute-done.20
  618.5 4.2 collective-permute-done.33
  (163 shorter events, 85.5 us)
Async XLA Ops:
  2.2 20.4 %copy-start.22 = (s32[1024]{0:T(1024)}, s32[1024]{0:T(1024)S(1)}, u32[]{:S(2)}) copy-start(s32[1024]{0:T(1024)S(1)} %select_reduce_fusion) | copy-start | bytes 12292
  50.2 4.5 collective-permute-start
  64.1 26.5 %collective-permute-start.1 = (bf16[256,2048]{1,0:T(8,128)(2,1)}, bf16[256,2048]{1,0:T(8,128)(2,1)S(1)}, u32[]{:S(2)}, u32[]{:S(2)}) collective-permute-start(bf16[256,2048]{1,0:T(8,128)(2,1)} %get-tuple-element.59), channel_id=1, source_target_pairs={{0,2},{1,3},{2,0},{3,1},{4,6},{5,7},{6,4},{7,5},{8,10},{9,11},{10,... | collective-permute-start | bytes 3145736 | tf_op jit(solution)/shard_map/ppermute | solution.py:293
  95.8 24.9 %collective-permute-start.3 = (bf16[256,2048]{1,0:T(8,128)(2,1)}, bf16[256,2048]{1,0:T(8,128)(2,1)S(1)}, u32[]{:S(2)}, u32[]{:S(2)}) collective-permute-start(bf16[256,2048]{1,0:T(8,128)(2,1)} %get-tuple-element.61.refs_0_), channel_id=1, source_target_pairs={{0,2},{1,3},{2,0},{3,1},{4,6},{5,7},{6,4},{7,5},{8,10},{9,11},{10,... | collective-permute-start | bytes 3145736 | tf_op jit(solution)/shard_map/ppermute | solution.py:293
  97.6 23.2 %collective-permute-start.2 = (bf16[256,2048]{1,0:T(8,128)(2,1)}, bf16[256,2048]{1,0:T(8,128)(2,1)S(1)}, u32[]{:S(2)}, u32[]{:S(2)}) collective-permute-start(bf16[256,2048]{1,0:T(8,128)(2,1)} %get-tuple-element.61.refs_0_), channel_id=1, source_target_pairs={{0,1},{1,0},{2,3},{3,2},{4,5},{5,4},{6,7},{7,6},{8,9},{9,8},{10,11... | collective-permute-start | bytes 3145736 | tf_op jit(solution)/shard_map/ppermute | solution.py:293
  120.7 2.7 collective-permute-start.4
  168.3 8.1 %collective-permute-start.5 = (bf16[2,256,2048]{2,1,0:T(8,128)(2,1)}, bf16[2,256,2048]{2,1,0:T(8,128)(2,1)S(1)}, u32[]{:S(2)}, u32[]{:S(2)}) collective-permute-start(bf16[2,256,2048]{2,1,0:T(8,128)(2,1)} %rows_send.5.refs_2_), channel_id=1, source_target_pairs={{0,1},{1,0},{2,3},{3,2},{4,5},{5,4},{6,7},{7,6},{8,9},{9,8},{10,11... | collective-permute-start | bytes 6291464 | tf_op jit(solution)/shard_map/ppermute | solution.py:293
  199.8 13.3 %copy-start.3 = (bf16[4,256,1408]{2,1,0:T(8,128)(2,1)S(1)}, bf16[4,256,1408]{2,1,0:T(8,128)(2,1)}, u32[]{:S(2)}) copy-start(bf16[4,256,1408]{2,1,0:T(8,128)(2,1)} %weight_send.9.refs_2_.refs_3_) | copy-start | bytes 8650756
  209.8 4.9 collective-permute-start.6
  210.1 65.6 %collective-permute-start.12 = (bf16[4,1408,256]{2,1,0:T(8,128)(2,1)}, bf16[4,1408,256]{2,1,0:T(8,128)(2,1)}, u32[]{:S(2)}, u32[]{:S(2)}) collective-permute-start(bf16[4,1408,256]{2,1,0:T(8,128)(2,1)} %weight_send.7.refs_3_), channel_id=1, source_target_pairs={{0,4},{4,0},{8,12},{12,8},{16,20},{20,16},{24,28},{28,24},{1,5},{5... | collective-permute-start | bytes 8650760 | tf_op jit(solution)/shard_map/ppermute | solution.py:293
  211.6 25.1 %collective-permute-start.8 = (bf16[256,2048]{1,0:T(8,128)(2,1)}, bf16[256,2048]{1,0:T(8,128)(2,1)S(1)}, u32[]{:S(2)}, u32[]{:S(2)}) collective-permute-start(bf16[256,2048]{1,0:T(8,128)(2,1)} %get-tuple-element.70), channel_id=1, source_target_pairs={{0,2},{1,3},{2,0},{3,1},{4,6},{5,7},{6,4},{7,5},{8,10},{9,11},{10,... | collective-permute-start | bytes 3145736 | tf_op jit(solution)/shard_map/ppermute | solution.py:293
  213.1 111.4 %collective-permute-start.13 = (bf16[4,256,1408]{2,1,0:T(8,128)(2,1)S(1)}, bf16[4,256,1408]{2,1,0:T(8,128)(2,1)}, u32[]{:S(2)}, u32[]{:S(2)}) collective-permute-start(bf16[4,256,1408]{2,1,0:T(8,128)(2,1)S(1)} %copy-done.3), channel_id=1, source_target_pairs={{0,8},{4,12},{8,0},{12,4},{16,24},{20,28},{24,16},{28,20},{1,9},{5... | collective-permute-start | bytes 8650760 | tf_op jit(solution)/shard_map/ppermute | solution.py:293
  243.2 24.4 %collective-permute-start.10 = (bf16[256,2048]{1,0:T(8,128)(2,1)}, bf16[256,2048]{1,0:T(8,128)(2,1)S(1)}, u32[]{:S(2)}, u32[]{:S(2)}) collective-permute-start(bf16[256,2048]{1,0:T(8,128)(2,1)} %get-tuple-element.72.refs_3_.refs_0_), channel_id=1, source_target_pairs={{0,2},{1,3},{2,0},{3,1},{4,6},{5,7},{6,4},{7,5},{8,10},{9,11},{10,... | collective-permute-start | bytes 3145736 | tf_op jit(solution)/shard_map/ppermute | solution.py:293
  244.7 41.4 %collective-permute-start.9 = (bf16[256,2048]{1,0:T(8,128)(2,1)}, bf16[256,2048]{1,0:T(8,128)(2,1)}, u32[]{:S(2)}, u32[]{:S(2)}) collective-permute-start(bf16[256,2048]{1,0:T(8,128)(2,1)} %get-tuple-element.72.refs_3_.refs_0_), channel_id=1, source_target_pairs={{0,1},{1,0},{2,3},{3,2},{4,5},{5,4},{6,7},{7,6},{8,9},{9,8},{10,11... | collective-permute-start | bytes 3145736 | tf_op jit(solution)/shard_map/ppermute | solution.py:293
  244.7 130.5 %collective-permute-start.16 = (bf16[4,256,1408]{2,1,0:T(8,128)(2,1)}, bf16[4,256,1408]{2,1,0:T(8,128)(2,1)}, u32[]{:S(2)}, u32[]{:S(2)}) collective-permute-start(bf16[4,256,1408]{2,1,0:T(8,128)(2,1)} %weight_send.8.refs_4_), channel_id=1, source_target_pairs={{0,4},{4,0},{8,12},{12,8},{16,20},{20,16},{24,28},{28,24},{1,5},{5... | collective-permute-start | bytes 8650760 | tf_op jit(solution)/shard_map/ppermute | solution.py:293
  267.6 18.5 %copy-start.17 = (bf16[256,2048]{1,0:T(8,128)(2,1)}, bf16[256,2048]{1,0:T(8,128)(2,1)S(1)}, u32[]{:S(2)}) copy-start(bf16[256,2048]{1,0:T(8,128)(2,1)S(1)} %collective-permute-done.10.refs_2_) | copy-start | bytes 3145732
  267.6 20.2 %collective-permute-start.11 = (bf16[256,2048]{1,0:T(8,128)(2,1)S(1)}, bf16[256,2048]{1,0:T(8,128)(2,1)}, u32[]{:S(2)}, u32[]{:S(2)}) collective-permute-start(bf16[256,2048]{1,0:T(8,128)(2,1)S(1)} %collective-permute-done.10.refs_2_), channel_id=1, source_target_pairs={{0,1},{1,0},{2,3},{3,2},{4,5},{5,4},{6,7},{7,6},{8,9},{9,8},{10,11... | collective-permute-start | bytes 3145736 | tf_op jit(solution)/shard_map/ppermute | solution.py:293
  275.8 86.2 %collective-permute-start.7 = (bf16[256,2048]{1,0:T(8,128)(2,1)}, bf16[256,2048]{1,0:T(8,128)(2,1)}, u32[]{:S(2)}, u32[]{:S(2)}) collective-permute-start(bf16[256,2048]{1,0:T(8,128)(2,1)} %get-tuple-element.69), channel_id=1, source_target_pairs={{0,2},{1,3},{2,0},{3,1},{4,6},{5,7},{6,4},{7,5},{8,10},{9,11},{10,... | collective-permute-start | bytes 3145736 | tf_op jit(solution)/shard_map/ppermute | solution.py:293
  286.1 81.6 %collective-permute-start.38 = (bf16[2,1408,256]{2,1,0:T(8,128)(2,1)}, bf16[2,1408,256]{2,1,0:T(8,128)(2,1)}, u32[]{:S(2)}, u32[]{:S(2)}) collective-permute-start(bf16[2,1408,256]{2,1,0:T(8,128)(2,1)} %get-tuple-element.73.refs_5_), channel_id=1, source_target_pairs={{0,8},{4,12},{8,0},{12,4},{16,24},{20,28},{24,16},{28,20},{1,9},{5... | collective-permute-start | bytes 4325384 | tf_op jit(solution)/shard_map/ppermute | solution.py:293
  350.2 10.4 %copy-start.4 = (bf16[1024,512]{1,0:T(8,128)(2,1)S(1)}, bf16[1024,512]{1,0:T(8,128)(2,1)}, u32[]{:S(2)}) copy-start(bf16[1024,512]{1,0:T(8,128)(2,1)} %get-tuple-element.57) | copy-start | bytes 3145732
  360.6 31.2 %collective-permute-start.14 = (bf16[2,256,2048]{2,1,0:T(8,128)(2,1)}, bf16[2,256,2048]{2,1,0:T(8,128)(2,1)}, u32[]{:S(2)}, u32[]{:S(2)}) collective-permute-start(bf16[2,256,2048]{2,1,0:T(8,128)(2,1)} %rows_send.7.refs_5_.refs_3_), channel_id=1, source_target_pairs={{0,1},{1,0},{2,3},{3,2},{4,5},{5,4},{6,7},{7,6},{8,9},{9,8},{10,11... | collective-permute-start | bytes 6291464 | tf_op jit(solution)/shard_map/ppermute | solution.py:293
  366.2 36.7 %collective-permute-start.34 = (bf16[2,256,1408]{2,1,0:T(8,128)(2,1)}, bf16[2,256,1408]{2,1,0:T(8,128)(2,1)}, u32[]{:S(2)}, u32[]{:S(2)}) collective-permute-start(bf16[2,256,1408]{2,1,0:T(8,128)(2,1)} %get-tuple-element.80.refs_2_), channel_id=1, source_target_pairs={{0,4},{4,0},{8,12},{12,8},{16,20},{20,16},{24,28},{28,24},{1,5},{5... | collective-permute-start | bytes 4325384 | tf_op jit(solution)/shard_map/ppermute | solution.py:293
  372.1 88.2 %collective-permute-start.39 = (bf16[1,1408,256]{2,1,0:T(8,128)(2,1)}, bf16[1,1408,256]{2,1,0:T(8,128)(2,1)}, u32[]{:S(2)}, u32[]{:S(2)}) collective-permute-start(bf16[1,1408,256]{2,1,0:T(8,128)(2,1)} %dynamic-slice_convert_fusion), channel_id=1, source_target_pairs={{0,16},{4,20},{8,24},{12,28},{16,0},{20,4},{24,8},{28,12},{1,17},{... | collective-permute-start | bytes 2162696 | tf_op jit(solution)/shard_map/ppermute | solution.py:293
  374.7 166.9 %collective-permute-start.24 = (bf16[4,256,512]{2,1,0:T(8,128)(2,1)S(1)}, bf16[4,256,512]{2,1,0:T(8,128)(2,1)}, u32[]{:S(2)}, u32[]{:S(2)}) collective-permute-start(bf16[4,256,512]{2,1,0:T(8,128)(2,1)S(1)} %copy-done.8), channel_id=1, source_target_pairs={{0,4},{4,0},{8,12},{12,8},{16,20},{20,16},{24,28},{28,24},{1,5},{5... | collective-permute-start | bytes 3145736 | tf_op jit(solution)/shard_map/ppermute | solution.py:293
  384.4 49.2 %collective-permute-start.36 = (bf16[2,256,1408]{2,1,0:T(8,128)(2,1)}, bf16[2,256,1408]{2,1,0:T(8,128)(2,1)}, u32[]{:S(2)}, u32[]{:S(2)}) collective-permute-start(bf16[2,256,1408]{2,1,0:T(8,128)(2,1)} %get-tuple-element.83.refs_5_), channel_id=1, source_target_pairs={{0,8},{4,12},{8,0},{12,4},{16,24},{20,28},{24,16},{28,20},{1,9},{5... | collective-permute-start | bytes 4325384 | tf_op jit(solution)/shard_map/ppermute | solution.py:293
  402.4 24.1 %collective-permute-start.15 = (bf16[256,2048]{1,0:T(8,128)(2,1)}, bf16[256,2048]{1,0:T(8,128)(2,1)}, u32[]{:S(2)}, u32[]{:S(2)}) collective-permute-start(bf16[256,2048]{1,0:T(8,128)(2,1)} %get-tuple-element.82), channel_id=1, source_target_pairs={{0,2},{1,3},{2,0},{3,1},{4,6},{5,7},{6,4},{7,5},{8,10},{9,11},{10,... | collective-permute-start | bytes 3145736 | tf_op jit(solution)/shard_map/ppermute | solution.py:293
  402.9 132.6 %collective-permute-start.21 = (bf16[4,256,512]{2,1,0:T(8,128)(2,1)}, bf16[4,256,512]{2,1,0:T(8,128)(2,1)}, u32[]{:S(2)}, u32[]{:S(2)}) collective-permute-start(bf16[4,256,512]{2,1,0:T(8,128)(2,1)} %weight_send.11.refs_2_), channel_id=1, source_target_pairs={{0,4},{4,0},{8,12},{12,8},{16,20},{20,16},{24,28},{28,24},{1,5},{5... | collective-permute-start | bytes 3145736 | tf_op jit(solution)/shard_map/ppermute | solution.py:293
  426.4 39.2 %collective-permute-start.35 = (bf16[1,256,1408]{2,1,0:T(8,128)(2,1)}, bf16[1,256,1408]{2,1,0:T(8,128)(2,1)}, u32[]{:S(2)}, u32[]{:S(2)}) collective-permute-start(bf16[1,256,1408]{2,1,0:T(8,128)(2,1)} %dynamic-slice_convert_fusion.2), channel_id=1, source_target_pairs={{0,16},{4,20},{8,24},{12,28},{16,0},{20,4},{24,8},{28,12},{1,17},{... | collective-permute-start | bytes 2162696 | tf_op jit(solution)/shard_map/ppermute | solution.py:293
  433.6 12.4 %collective-permute-start.27 = (f32[7,2048]{1,0:T(8,128)S(1)}, f32[7,2048]{1,0:T(8,128)S(1)}, u32[]{:S(2)}, u32[]{:S(2)}) collective-permute-start(f32[7,2048]{1,0:T(8,128)S(1)} %pad_maximum_fusion.2), channel_id=1, source_target_pairs={{0,4},{4,0},{8,12},{12,8},{16,20},{20,16},{24,28},{28,24},{1,5},{5... | collective-permute-start | bytes 172040 | tf_op jit(solution)/shard_map/ppermute | solution.py:293
  435.1 11.0 %copy-start.24 = (f32[2,2048]{1,0:T(2,128)S(1)}, f32[2,2048]{1,0:T(2,128)}, u32[]{:S(2)}) copy-start(f32[2,2048]{1,0:T(2,128)} %get-tuple-element.93) | copy-start | bytes 49156
  435.1 28.2 %copy-start.6 = (f32[2,1408,256]{2,1,0:T(8,128)S(1)}, f32[2,1408,256]{2,1,0:T(8,128)}, u32[]{:S(2)}) copy-start(f32[2,1408,256]{2,1,0:T(8,128)} %copy-done.5) | copy-start | bytes 8650756
  446.1 14.2 %collective-permute-start.28 = (f32[7,2048]{1,0:T(8,128)S(1)}, f32[7,2048]{1,0:T(8,128)S(1)}, u32[]{:S(2)}, u32[]{:S(2)}) collective-permute-start(f32[7,2048]{1,0:T(8,128)S(1)} %fusion.9), channel_id=1, source_target_pairs={{0,8},{4,12},{8,0},{12,4},{16,24},{20,28},{24,16},{28,20},{1,9},{5... | collective-permute-start | bytes 172040 | tf_op jit(solution)/shard_map/ppermute | solution.py:293
  446.6 49.8 %copy-start.18 = (bf16[4,512,256]{2,1,0:T(8,128)(2,1)S(1)}, bf16[4,512,256]{2,1,0:T(8,128)(2,1)}, u32[]{:S(2)}) copy-start(bf16[4,512,256]{2,1,0:T(8,128)(2,1)} %weight_send.13) | copy-start | bytes 3145732
  460.2 38.9 %collective-permute-start.37 = (bf16[1,256,1408]{2,1,0:T(8,128)(2,1)S(1)}, bf16[1,256,1408]{2,1,0:T(8,128)(2,1)S(1)}, u32[]{:S(2)}, u32[]{:S(2)}) collective-permute-start(bf16[1,256,1408]{2,1,0:T(8,128)(2,1)S(1)} %dynamic-slice_convert_fusion.1), channel_id=1, source_target_pairs={{0,16},{4,20},{8,24},{12,28},{16,0},{20,4},{24,8},{28,12},{1,17},{... | collective-permute-start | bytes 2162696 | tf_op jit(solution)/shard_map/ppermute | solution.py:293
  460.3 36.2 %collective-permute-start.29 = (f32[7,2048]{1,0:T(8,128)S(1)}, f32[7,2048]{1,0:T(8,128)S(1)}, u32[]{:S(2)}, u32[]{:S(2)}) collective-permute-start(f32[7,2048]{1,0:T(8,128)S(1)} %add.127), channel_id=1, source_target_pairs={{0,16},{4,20},{8,24},{12,28},{16,0},{20,4},{24,8},{28,12},{1,17},{... | collective-permute-start | bytes 172040 | tf_op jit(solution)/shard_map/ppermute | solution.py:293
  465.6 61.9 %collective-permute-start.17 = (bf16[4,256,512]{2,1,0:T(8,128)(2,1)}, bf16[4,256,512]{2,1,0:T(8,128)(2,1)}, u32[]{:S(2)}, u32[]{:S(2)}) collective-permute-start(bf16[4,256,512]{2,1,0:T(8,128)(2,1)} %weight_send.10.refs_2_), channel_id=1, source_target_pairs={{0,4},{4,0},{8,12},{12,8},{16,20},{20,16},{24,28},{28,24},{1,5},{5... | collective-permute-start | bytes 3145736 | tf_op jit(solution)/shard_map/ppermute | solution.py:293
  496.4 25.2 %collective-permute-start.18 = (bf16[4,512,256]{2,1,0:T(8,128)(2,1)S(1)}, bf16[4,512,256]{2,1,0:T(8,128)(2,1)}, u32[]{:S(2)}, u32[]{:S(2)}) collective-permute-start(bf16[4,512,256]{2,1,0:T(8,128)(2,1)S(1)} %copy-done.18), channel_id=1, source_target_pairs={{0,4},{4,0},{8,12},{12,8},{16,20},{20,16},{24,28},{28,24},{1,5},{5... | collective-permute-start | bytes 3145736 | tf_op jit(solution)/shard_map/ppermute | solution.py:293
  499.2 1.3 collective-permute-start.30
  500.5 49.0 %collective-permute-start.31 = (f32[7,2048]{1,0:T(8,128)S(1)}, f32[7,2048]{1,0:T(8,128)S(1)}, u32[]{:S(2)}, u32[]{:S(2)}) collective-permute-start(f32[7,2048]{1,0:T(8,128)S(1)} %add.129), channel_id=1, source_target_pairs={{0,2},{1,3},{2,0},{3,1},{4,6},{5,7},{6,4},{7,5},{8,10},{9,11},{10,... | collective-permute-start | bytes 172040 | tf_op jit(solution)/shard_map/ppermute | solution.py:293
  527.5 52.9 %collective-permute-start.32 = (bf16[2,512,256]{2,1,0:T(8,128)(2,1)}, bf16[2,512,256]{2,1,0:T(8,128)(2,1)S(1)}, u32[]{:S(2)}, u32[]{:S(2)}) collective-permute-start(bf16[2,512,256]{2,1,0:T(8,128)(2,1)} %get-tuple-element.86.refs_3_), channel_id=1, source_target_pairs={{0,8},{4,12},{8,0},{12,4},{16,24},{20,28},{24,16},{28,20},{1,9},{5... | collective-permute-start | bytes 1572872 | tf_op jit(solution)/shard_map/ppermute | solution.py:293
  533.5 45.7 %collective-permute-start.19 = (bf16[2,256,512]{2,1,0:T(8,128)(2,1)}, bf16[2,256,512]{2,1,0:T(8,128)(2,1)S(1)}, u32[]{:S(2)}, u32[]{:S(2)}) collective-permute-start(bf16[2,256,512]{2,1,0:T(8,128)(2,1)} %get-tuple-element.88.refs_3_), channel_id=1, source_target_pairs={{0,8},{4,12},{8,0},{12,4},{16,24},{20,28},{24,16},{28,20},{1,9},{5... | collective-permute-start | bytes 1572872 | tf_op jit(solution)/shard_map/ppermute | solution.py:293
  541.5 35.3 %collective-permute-start.22 = (bf16[2,256,512]{2,1,0:T(8,128)(2,1)}, bf16[2,256,512]{2,1,0:T(8,128)(2,1)S(1)}, u32[]{:S(2)}, u32[]{:S(2)}) collective-permute-start(bf16[2,256,512]{2,1,0:T(8,128)(2,1)} %get-tuple-element.90.refs_3_), channel_id=1, source_target_pairs={{0,8},{4,12},{8,0},{12,4},{16,24},{20,28},{24,16},{28,20},{1,9},{5... | collective-permute-start | bytes 1572872 | tf_op jit(solution)/shard_map/ppermute | solution.py:293
  547.5 29.3 %copy-start.16 = (f32[2,256,512]{2,1,0:T(8,128)S(1)}, f32[2,256,512]{2,1,0:T(8,128)}, u32[]{:S(2)}) copy-start(f32[2,256,512]{2,1,0:T(8,128)} %get-tuple-element.89) | copy-start | bytes 3145732
  547.5 26.9 %collective-permute-start.25 = (bf16[2,256,512]{2,1,0:T(8,128)(2,1)}, bf16[2,256,512]{2,1,0:T(8,128)(2,1)S(1)}, u32[]{:S(2)}, u32[]{:S(2)}) collective-permute-start(bf16[2,256,512]{2,1,0:T(8,128)(2,1)} %get-tuple-element.92), channel_id=1, source_target_pairs={{0,8},{4,12},{8,0},{12,4},{16,24},{20,28},{24,16},{28,20},{1,9},{5... | collective-permute-start | bytes 1572872 | tf_op jit(solution)/shard_map/ppermute | solution.py:293
  575.9 30.0 %collective-permute-start.26 = (bf16[1,256,512]{2,1,0:T(8,128)(2,1)S(1)}, bf16[1,256,512]{2,1,0:T(8,128)(2,1)S(1)}, u32[]{:S(2)}, u32[]{:S(2)}) collective-permute-start(bf16[1,256,512]{2,1,0:T(8,128)(2,1)S(1)} %dynamic-slice_convert_fusion.4), channel_id=1, source_target_pairs={{0,16},{4,20},{8,24},{12,28},{16,0},{20,4},{24,8},{28,12},{1,17},{... | collective-permute-start | bytes 786440 | tf_op jit(solution)/shard_map/ppermute | solution.py:293
  577.1 34.4 %collective-permute-start.23 = (bf16[1,256,512]{2,1,0:T(8,128)(2,1)S(1)}, bf16[1,256,512]{2,1,0:T(8,128)(2,1)S(1)}, u32[]{:S(2)}, u32[]{:S(2)}) collective-permute-start(bf16[1,256,512]{2,1,0:T(8,128)(2,1)S(1)} %dynamic-slice_convert_fusion.5), channel_id=1, source_target_pairs={{0,16},{4,20},{8,24},{12,28},{16,0},{20,4},{24,8},{28,12},{1,17},{... | collective-permute-start | bytes 786440 | tf_op jit(solution)/shard_map/ppermute | solution.py:293
  579.4 37.7 %collective-permute-start.20 = (bf16[1,256,512]{2,1,0:T(8,128)(2,1)S(1)}, bf16[1,256,512]{2,1,0:T(8,128)(2,1)S(1)}, u32[]{:S(2)}, u32[]{:S(2)}) collective-permute-start(bf16[1,256,512]{2,1,0:T(8,128)(2,1)S(1)} %dynamic-slice_convert_fusion.6), channel_id=1, source_target_pairs={{0,16},{4,20},{8,24},{12,28},{16,0},{20,4},{24,8},{28,12},{1,17},{... | collective-permute-start | bytes 786440 | tf_op jit(solution)/shard_map/ppermute | solution.py:293
  580.5 42.1 %collective-permute-start.33 = (bf16[1,512,256]{2,1,0:T(8,128)(2,1)S(1)}, bf16[1,512,256]{2,1,0:T(8,128)(2,1)S(1)}, u32[]{:S(2)}, u32[]{:S(2)}) collective-permute-start(bf16[1,512,256]{2,1,0:T(8,128)(2,1)S(1)} %dynamic-slice_convert_fusion.3), channel_id=1, source_target_pairs={{0,16},{4,20},{8,24},{12,28},{16,0},{20,4},{24,8},{28,12},{1,17},{... | collective-permute-start | bytes 786440 | tf_op jit(solution)/shard_map/ppermute | solution.py:293
  (17 other events, 52.2 us)
